TPU v7x, 32 devices: a whole 2x2x4 slice. The times are simulated.
32 devices in a mesh: seq: 8 (over y, x, core), head: 4 (over z).
Axes of the slice: x: 2, y: 2, z: 4, core: 2. Of those that a mesh axis runs over, the one named last changes fastest.
Arguments:
- stream: float32 [2, 8192, 1024], P(None, 'seq'), may hold values from -20 to 20
- cotangent: float32 [2, 8192, 1024], P(None, 'seq'), may hold values from -6 to 6
- mixer_in: bfloat16 [1024, 4, 1024], P(None, None, 'head'), may hold values from -0.1875 to 0.1875
- memory_in: bfloat16 [1024, 3, 1024], P(None, None, 'head'), may hold values from -0.1875 to 0.1875
- mixer_out: bfloat16 [1024, 1024], P('head'), may hold values from -0.5 to 0.5
- ffn_in: bfloat16 [1024, 2, 2816], P(None, None, 'head'), may hold values from -0.1875 to 0.1875
- ffn_out: bfloat16 [2816, 1024], P('head'), may hold values from -0.109375 to 0.109375
- persistent: bfloat16 [32, 1024], P(None, 'head'), may hold values from -5 to 5
- norm_gains: float32 [2, 1024], replicated, may hold values from 0.1 to 1.9
- conv_weight: float32 [4, 1024], replicated, may hold values from -3 to 3
- decays: float32 [2, 8, 8192], P(None, 'head', 'seq'), may hold values from 0 to 1
- doc_starts: int32 [2, 8], replicated, may hold values from 1 to 8192, as said below
Outputs:
- result: float32 [2, 8192, 1024], P(None, 'seq', 'head')
- grad_stream: float32 [2, 8192, 1024], P(None, 'seq', 'head')
- grad_mixer_in: float32 [1024, 4, 1024], P('seq', None, 'head')
- grad_memory_in: float32 [1024, 3, 1024], P('seq', None, 'head')
- grad_mixer_out: float32 [1024, 1024], P('head', 'seq')
- grad_ffn_in: float32 [1024, 2, 2816], P('seq', None, 'head')
- grad_ffn_out: float32 [2816, 1024], P('head', 'seq')
- grad_persistent: float32 [32, 1024], P('seq', 'head')
- grad_norm_gains: float32 [2, 1024], replicated
- grad_conv_weight: float32 [4, 1024], replicated
- rms_values: float32 [4], replicated
Inputs may be any that keep to these rules, and one draw needn't show every extreme that they name: `doc_starts`: in each stream either every entry equals 8192, so that the whole stream is one document, or the entries are strictly increasing and entry k lies in the k-th of 8 equal stretches of the stream; position 0 always begins a document.
All inputs are finite; a program needn't handle non-finite values.
Results may differ from a plain program's by a relative error of at most 0.012.
The roundings to bfloat16 on the way count: a program that leaves them out, or rounds other values in their place, can miss the bound.
Values may be sent and summed in bfloat16 or wider, within the bound.
No kernel may reach another device: no remote copies, remote signals or barrier semaphores. Data moves between devices by JAX's collectives and lax.ppermute only.
A program may use at most 256 MiB of HBM per device.

v0:
```python
import jax
import jax.numpy as jnp
from jax import lax
from jax.sharding import PartitionSpec as P

HD = 128


EPS = 1e-06
HIGH = lax.Precision.HIGHEST


def passed_along(value, axis, steps):
    count = lax.axis_size(axis)
    initial, last = (max(0, -steps), min(count, count - steps))
    return lax.ppermute(value, axis, [(source, source + steps) for source in range(initial, last)])


def carried_in(part, axis, combine, identity, reverse):
    count = lax.axis_size(axis)
    place = lax.axis_index(axis)
    ahead = count - 1 - place if reverse else place
    gathered = jax.tree.map(lambda a: lax.all_gather(a, axis), part)
    state = jax.tree.map(lambda a, e: jnp.zeros_like(a) + jnp.asarray(e, a.dtype), part, identity)

    def one(step, state):
        source = count - 1 - step if reverse else step
        return combine(
            state, jax.tree.map(lambda a: lax.dynamic_index_in_dim(a, source, 0, False), gathered)
        )

    return lax.fori_loop(0, ahead, one, state)


def doc_index(doc_starts, positions):
    return jnp.sum((doc_starts[:, None, :] <= positions[None, :, None]).astype(jnp.int32), axis=-1)


def split_heads(values, head_count):
    return jnp.transpose(
        values.reshape(values.shape[0], values.shape[1], head_count, HD), (0, 2, 1, 3)
    )


def join_heads(values):
    return jnp.transpose(values, (0, 2, 1, 3)).reshape(
        values.shape[0], values.shape[2], values.shape[1] * values.shape[3]
    )


def combine_states(earlier, following):
    return (earlier[0] * following[0], following[0][..., None, None] * earlier[1] + following[1])


def unit_back(raw_rows, inv_len, grad_rows):
    unit_vals = raw_rows * inv_len
    return inv_len * (
        grad_rows - unit_vals * jnp.sum(unit_vals * grad_rows, axis=-1, keepdims=True)
    )


def norm_back(values, inv_len, gain_row, grad_rows):
    hat_rows = values * inv_len
    scaled = grad_rows * gain_row
    grad_values = inv_len * (
        scaled - hat_rows * jnp.mean(scaled * hat_rows, axis=-1, keepdims=True)
    )
    return (grad_values, jnp.sum(grad_rows * hat_rows, axis=(0, 1)))


def attention_scores(queries, keys_seg, per_keys, allowed, score_scale):
    seg_scores = score_scale * jnp.einsum(
        "bhtc,bhsc->bhts", queries, keys_seg, preferred_element_type=jnp.float32
    )
    seg_scores = jnp.where(allowed[:, None], seg_scores, -1e30)
    per_scores = score_scale * jnp.einsum(
        "bhtc,phc->bhtp", queries, per_keys, preferred_element_type=jnp.float32
    )
    return (seg_scores, per_scores)


def local(
    stream,
    cotangent,
    mixer_in,
    memory_in,
    mixer_out,
    ffn_in,
    ffn_out,
    persistent,
    norm_gains,
    conv_weight,
    decays,
    doc_starts,
):
    batch_rows, seg_len, model_width = stream.shape
    head_count = mixer_out.shape[0] // HD
    tap_count = conv_weight.shape[0]
    rim_len = tap_count - 1
    persist_rows = persistent.shape[0] // 2
    score_scale = HD ** (-0.5)
    first_pos = lax.axis_index("seq") * seg_len
    positions = first_pos + jnp.arange(seg_len, dtype=jnp.int32)
    doc_ids = doc_index(doc_starts, positions)
    rim_ids = doc_index(doc_starts, first_pos - rim_len + jnp.arange(rim_len, dtype=jnp.int32))
    prev_ids = doc_index(doc_starts, jnp.reshape(first_pos - 1, (1,)))
    col_share = model_width // lax.axis_size("head")
    col_start = lax.axis_index("head") * col_share
    allowed = (positions[:, None] >= positions[None, :])[None] & (
        doc_ids[:, :, None] == doc_ids[:, None, :]
    )
    stream_cols = lax.dynamic_slice_in_dim(stream, col_start, col_share, 2)
    inv_one = lax.rsqrt(jnp.mean(stream * stream, axis=-1, keepdims=True) + EPS)
    normed = (stream * inv_one * norm_gains[0]).astype(jnp.bfloat16)
    rim_rows = passed_along(normed[:, seg_len - rim_len :], "seq", 1)
    extended = jnp.concatenate([rim_rows, normed], axis=1).astype(jnp.float32)
    ext_ids = jnp.concatenate([rim_ids, doc_ids], axis=1)
    tap_masks = []
    conv_sum = jnp.zeros(stream.shape, jnp.float32)
    for tap_index in range(tap_count):
        lead_row = rim_len - tap_index
        same_doc = (ext_ids[:, lead_row : lead_row + seg_len] == doc_ids)[..., None]
        tap_masks.append(same_doc)
        conv_sum = (
            conv_sum
            + jnp.where(same_doc, extended[:, lead_row : lead_row + seg_len], 0.0)
            * conv_weight[tap_index]
        )
    conv_out = conv_sum.astype(jnp.bfloat16)
    projected = jnp.einsum("btd,dkc->btkc", normed, mixer_in, preferred_element_type=jnp.float32)
    queries = split_heads(projected[:, :, 0].astype(jnp.bfloat16), head_count)
    keys_seg = split_heads(projected[:, :, 1].astype(jnp.bfloat16), head_count)
    values_seg = split_heads(projected[:, :, 2].astype(jnp.bfloat16), head_count)
    gate_open = split_heads(jax.nn.sigmoid(projected[:, :, 3]), head_count)
    per_keys = persistent[:persist_rows].reshape(persist_rows, head_count, HD)
    per_values = persistent[persist_rows:].reshape(persist_rows, head_count, HD)
    seg_scores, per_scores = attention_scores(queries, keys_seg, per_keys, allowed, score_scale)
    row_top = jnp.maximum(jnp.max(seg_scores, axis=-1), jnp.max(per_scores, axis=-1))[..., None]
    seg_exp = jnp.exp(seg_scores - row_top)
    per_exp = jnp.exp(per_scores - row_top)
    row_total = jnp.sum(seg_exp, axis=-1, keepdims=True) + jnp.sum(per_exp, axis=-1, keepdims=True)
    log_total = row_top + jnp.log(row_total)
    attended = jnp.einsum(
        "bhts,bhsc->bhtc",
        (seg_exp / row_total).astype(jnp.bfloat16),
        values_seg,
        preferred_element_type=jnp.float32,
    )
    attended = attended + jnp.einsum(
        "bhtp,phc->bhtc",
        (per_exp / row_total).astype(jnp.bfloat16),
        per_values,
        preferred_element_type=jnp.float32,
    )
    memory_proj = jnp.einsum(
        "btd,dkc->btkc", conv_out, memory_in, preferred_element_type=jnp.float32
    )
    query_raw = split_heads(memory_proj[:, :, 0], head_count)
    key_raw = split_heads(memory_proj[:, :, 1], head_count)
    query_inv = lax.rsqrt(jnp.sum(query_raw * query_raw, axis=-1, keepdims=True) + EPS)
    key_inv = lax.rsqrt(jnp.sum(key_raw * key_raw, axis=-1, keepdims=True) + EPS)
    mem_query = (query_raw * query_inv).astype(jnp.bfloat16)
    mem_key = (key_raw * key_inv).astype(jnp.bfloat16)
    mem_value = split_heads(memory_proj[:, :, 2].astype(jnp.bfloat16), head_count)
    value_wide = mem_value.astype(jnp.float32)
    log_sums = jnp.cumsum(jnp.log(decays), axis=-1)
    log_gaps = log_sums[..., :, None] - log_sums[..., None, :]
    decay_grid = jnp.where(allowed[:, None], jnp.exp(jnp.minimum(log_gaps, 0.0)), 0.0)
    mem_scores = jnp.einsum(
        "bhtc,bhsc->bhts", mem_query, mem_key, preferred_element_type=jnp.float32
    )
    mem_weights = (mem_scores * decay_grid).astype(jnp.bfloat16)
    recalled = jnp.einsum(
        "bhts,bhsc->bhtc", mem_weights, mem_value, preferred_element_type=jnp.float32
    )
    valid_rows = (doc_ids == prev_ids).astype(jnp.float32)
    inflow = jnp.exp(log_sums) * valid_rows[:, None, :]
    end_ids = doc_ids[:, seg_len - 1 :]
    keep_weights = (
        jnp.exp(log_sums[..., seg_len - 1 :] - log_sums)
        * (doc_ids == end_ids).astype(jnp.float32)[:, None, :]
    )
    carry_decay = jnp.exp(log_sums[..., seg_len - 1]) * (end_ids == prev_ids).astype(jnp.float32)
    kept_keys = mem_key.astype(jnp.float32) * keep_weights[..., None]
    local_state = jnp.einsum("bhsc,bhsd->bhcd", kept_keys, value_wide, precision=HIGH)
    identity = (jnp.ones_like(carry_decay), jnp.zeros_like(local_state))
    decay_in, state_in = carried_in(
        (carry_decay, local_state), "seq", combine_states, identity, False
    )
    in_queries = mem_query.astype(jnp.float32) * inflow[..., None]
    recalled = recalled + jnp.einsum("bhtc,bhcd->bhtd", in_queries, state_in, precision=HIGH)
    branch = (attended + gate_open * recalled).astype(jnp.bfloat16)
    flat_branch = join_heads(branch)
    mixed_part = jnp.einsum(
        "btc,cd->btd", flat_branch, mixer_out, preferred_element_type=jnp.float32
    )
    mixed_out = lax.psum(mixed_part, "head")
    middle = stream + mixed_out
    inv_two = lax.rsqrt(jnp.mean(middle * middle, axis=-1, keepdims=True) + EPS)
    normed_two = (middle * inv_two * norm_gains[1]).astype(jnp.bfloat16)
    mid_share = lax.dynamic_slice_in_dim(middle, col_start, col_share, 2)
    mixed_cols = lax.dynamic_slice_in_dim(mixed_out, col_start, col_share, 2)
    up_pair = jnp.einsum("btd,dkf->btkf", normed_two, ffn_in, preferred_element_type=jnp.float32)
    gate_pre = up_pair[:, :, 0]
    up_part = up_pair[:, :, 1]
    silu_gate = jax.nn.silu(gate_pre)
    hidden = (silu_gate * up_part).astype(jnp.bfloat16)
    ffn_part = jnp.einsum("btf,fd->btd", hidden, ffn_out, preferred_element_type=jnp.float32)
    ffn_share = lax.psum_scatter(
        ffn_part.astype(jnp.bfloat16), "head", scatter_dimension=2, tiled=True
    ).astype(jnp.float32)
    result = mid_share + ffn_share
    grad_ffn = cotangent.astype(jnp.bfloat16)
    grad_hidden = jnp.einsum("btd,fd->btf", grad_ffn, ffn_out, preferred_element_type=jnp.float32)
    gate_sigmoid = jax.nn.sigmoid(gate_pre)
    silu_slope = gate_sigmoid * (1.0 + gate_pre * (1.0 - gate_sigmoid))
    grad_gate_pre = (grad_hidden * up_part * silu_slope).astype(jnp.bfloat16)
    grad_up = (grad_hidden * silu_gate).astype(jnp.bfloat16)
    grad_pair = jnp.stack([grad_gate_pre, grad_up], axis=2)
    grad_ffn_in = jnp.einsum(
        "btd,btkf->dkf", normed_two, grad_pair, preferred_element_type=jnp.float32
    )
    grad_ffn_out = jnp.einsum("btf,btd->fd", hidden, grad_ffn, preferred_element_type=jnp.float32)
    grad_normed_two = jnp.einsum(
        "btkf,dkf->btd", grad_pair, ffn_in, preferred_element_type=jnp.float32
    )
    grad_norm_terms, grad_gain_two = norm_back(middle, inv_two, norm_gains[1], grad_normed_two)
    grad_norm_summed = lax.psum_scatter(grad_norm_terms, "head", scatter_dimension=2, tiled=True)
    grad_mid_share = grad_norm_summed + lax.dynamic_slice_in_dim(cotangent, col_start, col_share, 2)
    grad_mix = lax.all_gather(grad_mid_share.astype(jnp.bfloat16), "head", axis=2, tiled=True)
    grad_mixer_out = jnp.einsum(
        "btc,btd->cd", flat_branch, grad_mix, preferred_element_type=jnp.float32
    )
    grad_flat = jnp.einsum(
        "btd,cd->btc", grad_mix, mixer_out, preferred_element_type=jnp.float32
    ).astype(jnp.bfloat16)
    grad_branch = split_heads(grad_flat, head_count)
    grad_branch_wide = grad_branch.astype(jnp.float32)
    grad_gate = grad_branch_wide * recalled
    grad_recalled = (grad_branch_wide * gate_open).astype(jnp.bfloat16)
    grad_gate_mix = (grad_gate * gate_open * (1.0 - gate_open)).astype(jnp.bfloat16)
    seg_scores, per_scores = attention_scores(queries, keys_seg, per_keys, allowed, score_scale)
    seg_probs = jnp.exp(seg_scores - log_total)
    per_probs = jnp.exp(per_scores - log_total)
    seg_grad_probs = jnp.einsum(
        "bhtc,bhsc->bhts", grad_branch, values_seg, preferred_element_type=jnp.float32
    )
    per_grad_probs = jnp.einsum(
        "bhtc,phc->bhtp", grad_branch, per_values, preferred_element_type=jnp.float32
    )
    row_delta = jnp.sum(seg_probs * seg_grad_probs, axis=-1, keepdims=True) + jnp.sum(
        per_probs * per_grad_probs, axis=-1, keepdims=True
    )
    seg_grad_scores = (seg_probs * (seg_grad_probs - row_delta)).astype(jnp.bfloat16)
    per_grad_scores = (per_probs * (per_grad_probs - row_delta)).astype(jnp.bfloat16)
    grad_queries = score_scale * (
        jnp.einsum("bhts,bhsc->bhtc", seg_grad_scores, keys_seg, preferred_element_type=jnp.float32)
        + jnp.einsum(
            "bhtp,phc->bhtc", per_grad_scores, per_keys, preferred_element_type=jnp.float32
        )
    )
    grad_keys = score_scale * jnp.einsum(
        "bhts,bhtc->bhsc", seg_grad_scores, queries, preferred_element_type=jnp.float32
    )
    grad_per_keys = score_scale * jnp.einsum(
        "bhtp,bhtc->phc", per_grad_scores, queries, preferred_element_type=jnp.float32
    )
    grad_values = jnp.einsum(
        "bhts,bhtc->bhsc",
        seg_probs.astype(jnp.bfloat16),
        grad_branch,
        preferred_element_type=jnp.float32,
    )
    grad_per_values = jnp.einsum(
        "bhtp,bhtc->phc",
        per_probs.astype(jnp.bfloat16),
        grad_branch,
        preferred_element_type=jnp.float32,
    )
    grad_persistent = jnp.concatenate(
        [
            grad_per_keys.reshape(persist_rows, head_count * HD),
            grad_per_values.reshape(persist_rows, head_count * HD),
        ],
        axis=0,
    )
    recalled_wide = grad_recalled.astype(jnp.float32)
    state_terms = jnp.einsum("bhtc,bhtd->bhcd", in_queries, recalled_wide, precision=HIGH)
    decay_out, grad_state = carried_in(
        (carry_decay, state_terms), "seq", combine_states, identity, True
    )
    grad_weights = jnp.einsum(
        "bhtc,bhsc->bhts", grad_recalled, mem_value, preferred_element_type=jnp.float32
    )
    grad_mem_scores = (grad_weights * decay_grid).astype(jnp.bfloat16)
    grad_mem_query = jnp.einsum(
        "bhts,bhsc->bhtc", grad_mem_scores, mem_key, preferred_element_type=jnp.float32
    )
    grad_mem_query = grad_mem_query + inflow[..., None] * jnp.einsum(
        "bhtd,bhcd->bhtc", recalled_wide, state_in, precision=HIGH
    )
    grad_mem_key = jnp.einsum(
        "bhts,bhtc->bhsc", grad_mem_scores, mem_query, preferred_element_type=jnp.float32
    )
    grad_mem_key = grad_mem_key + keep_weights[..., None] * jnp.einsum(
        "bhsd,bhcd->bhsc", value_wide, grad_state, precision=HIGH
    )
    grad_mem_value = jnp.einsum(
        "bhts,bhtc->bhsc", mem_weights, grad_recalled, preferred_element_type=jnp.float32
    )
    grad_mem_value = grad_mem_value + jnp.einsum(
        "bhsc,bhcd->bhsd", kept_keys, grad_state, precision=HIGH
    )
    grad_query_raw = unit_back(query_raw, query_inv, grad_mem_query).astype(jnp.bfloat16)
    grad_key_raw = unit_back(key_raw, key_inv, grad_mem_key).astype(jnp.bfloat16)
    grad_mem_cat = jnp.stack(
        [
            join_heads(grad_query_raw),
            join_heads(grad_key_raw),
            join_heads(grad_mem_value.astype(jnp.bfloat16)),
        ],
        axis=2,
    )
    grad_memory_in = jnp.einsum(
        "btd,btkc->dkc", conv_out, grad_mem_cat, preferred_element_type=jnp.float32
    )
    grad_conv_out = jnp.einsum(
        "btkc,dkc->btd", grad_mem_cat, memory_in, preferred_element_type=jnp.float32
    )
    grad_mix_cat = jnp.stack(
        [
            join_heads(grad_queries.astype(jnp.bfloat16)),
            join_heads(grad_keys.astype(jnp.bfloat16)),
            join_heads(grad_values.astype(jnp.bfloat16)),
            join_heads(grad_gate_mix),
        ],
        axis=2,
    )
    grad_mixer_in = jnp.einsum(
        "btd,btkc->dkc", normed, grad_mix_cat, preferred_element_type=jnp.float32
    )
    grad_normed = jnp.einsum(
        "btkc,dkc->btd", grad_mix_cat, mixer_in, preferred_element_type=jnp.float32
    )
    grad_ext = jnp.zeros((batch_rows, seg_len + rim_len, model_width), jnp.float32)
    conv_terms = []
    for tap_index in range(tap_count):
        lead_row = rim_len - tap_index
        masked = jnp.where(tap_masks[tap_index], grad_conv_out, 0.0)
        conv_terms.append(jnp.sum(masked * extended[:, lead_row : lead_row + seg_len], axis=(0, 1)))
        grad_ext = grad_ext + jnp.pad(
            masked * conv_weight[tap_index], ((0, 0), (lead_row, tap_index), (0, 0))
        )
    grad_conv = jnp.stack(conv_terms)
    rim_grads = passed_along(grad_ext[:, :rim_len], "seq", -1)
    grad_normed = (
        grad_normed
        + grad_ext[:, rim_len:]
        + jnp.pad(rim_grads, ((0, 0), (seg_len - rim_len, 0), (0, 0)))
    )
    grad_in_part, grad_gain_one = norm_back(stream, inv_one, norm_gains[0], grad_normed)
    grad_stream = (
        lax.psum_scatter(grad_in_part, "head", scatter_dimension=2, tiled=True) + grad_mid_share
    )
    grad_mixer_in, grad_memory_in, grad_mixer_out, grad_ffn_in, grad_ffn_out, grad_persistent = (
        lax.psum_scatter(grad_mixer_in, "seq", scatter_dimension=0, tiled=True),
        lax.psum_scatter(grad_memory_in, "seq", scatter_dimension=0, tiled=True),
        lax.psum_scatter(grad_mixer_out, "seq", scatter_dimension=1, tiled=True),
        lax.psum_scatter(grad_ffn_in, "seq", scatter_dimension=0, tiled=True),
        lax.psum_scatter(grad_ffn_out, "seq", scatter_dimension=1, tiled=True),
        lax.psum_scatter(grad_persistent, "seq", scatter_dimension=0, tiled=True),
    )
    squares = jnp.stack(
        [
            jnp.sum(stream_cols * stream_cols),
            jnp.sum(mixed_cols * mixed_cols),
            jnp.sum(ffn_share * ffn_share),
            jnp.sum(result * result),
        ]
    )
    gains_total, conv_total, square_total = lax.psum(
        (jnp.stack([grad_gain_one, grad_gain_two]), grad_conv, squares), ("seq", "head")
    )
    cell_count = float(batch_rows * seg_len * lax.axis_size("seq") * model_width)
    rms_values = jnp.sqrt(square_total / cell_count)
    return (
        result,
        grad_stream,
        grad_mixer_in,
        grad_memory_in,
        grad_mixer_out,
        grad_ffn_in,
        grad_ffn_out,
        grad_persistent,
        gains_total,
        conv_total,
        rms_values,
    )


def solution(mesh):
    placed = (
        P(None, "seq", None),
        P(None, "seq", None),
        P(None, None, "head"),
        P(None, None, "head"),
        P("head", None),
        P(None, None, "head"),
        P("head", None),
        P(None, "head"),
        P(),
        P(),
        P(None, "head", "seq"),
        P(),
    )
    return jax.shard_map(
        local,
        mesh=mesh,
        in_specs=placed,
        out_specs=(
            P(None, "seq", "head"),
            P(None, "seq", "head"),
            P("seq", None, "head"),
            P("seq", None, "head"),
            P("head", "seq"),
            P("seq", None, "head"),
            P("head", "seq"),
            P("seq", "head"),
            P(),
            P(),
            P(),
        ),
        check_vma=False,
    )
```

profile of v0, /device:TPU:0, one launch (start us, length us, event | category | flops | bytes accessed | tf_op | source)
XLA Modules:
  0.0 1270.5 jit_solution(17860614711529828980)
XLA Ops:
  7.3 4.2 multiply_reduce_fusion.8
  16.0 2.4 collective-permute-start
  24.3 3.7 compare_and_fusion
  27.9 4.3 copy.376
  32.2 10.7 fusion.130
  50.9 11.6 fusion.131
  63.9 5.8 add_convert_fusion
  69.7 3.7 fusion.17
  80.2 9.9 all_gather.21
  90.2 8.1 fusion
  100.2 3.8 fusion.39
  104.1 5.7 multiply_convert_fusion.2
  109.8 3.2 copy-done.12
  113.0 2.6 fusion.139
  115.7 4.2 fusion.72
  120.0 8.7 fusion.52
  129.8 4.5 fusion.96
  134.4 298.7 %all-reduce.9.cloned.1.call-done = f32[2,1024,1024]{2,1,0:T(8,128)} async-done(((f32[2,1024,1024]{2,1,0:T(8,128)}), f32[2,1024,1024]{2,1,0:T(8,128)}) %all-reduce.9.cloned.1.call-update) | async-done | bytes 8388624 | tf_op jit(solution)/shard_map/psum | solution.py:197
  433.1 9.9 multiply_reduce_fusion.7
  443.1 12.8 %fusion.13 = f32[2,1024,2,704]{1,3,2,0:T(8,128)} fusion(bf16[1024,2,704]{0,2,1:T(8,128)(2,1)S(1)} %copy-done, f32[2,1024,1024]{2,1,0:T(8,128)} %get-tuple-element.243, f32[1024]{0:T(1024)S(1)} %bitcast.433, f32[2,1024]{1,0:T(2,128)S(1)} %add_rsqrt_fusion.2), kind=kOutput, calls=%fused_computation.57 | convolution fusion | flops 5911871488 | bytes 22818816 | tf_op jit(solution)/shard_map/btd,dkf->btkf/dot_general | solution.py:203
  455.9 12.6 fusion.29
  468.5 11.1 fusion.6
  479.6 4.1 subtract_multiply_fusion.1
  483.9 143.6 %reduce-scatter.11.cloned.1.call-done = f32[2,1024,256]{2,1,0:T(8,128)} async-done(((f32[2,1024,1024]{2,1,0:T(8,128)}), f32[2,1024,256]{2,1,0:T(8,128)}) %reduce-scatter.11.cloned.1.call-update) | async-done | bytes 2097168 | tf_op jit(solution)/shard_map/reduce_scatter | solution.py:228
  627.4 3.4 fusion.94
  631.4 80.9 %all-gather.6.cloned.1.call-done = bf16[2,1024,1024]{2,1,0:T(8,128)(2,1)} async-done(((bf16[2,1024,256]{2,1,0:T(8,128)(2,1)}), bf16[2,1024,1024]{2,1,0:T(8,128)(2,1)}) %all-gather.6.cloned.1.call-update) | async-done | bytes 4194320 | tf_op jit(solution)/shard_map/all_gather | solution.py:230
  712.3 3.5 convolution_convert_fusion.1
  715.8 2.3 multiply_convert_fusion.8
  721.2 7.7 convolution_convert_fusion
  730.1 2.3 fusion.137
  732.4 8.3 multiply_convert_fusion
  740.8 10.2 fusion.76
  751.0 6.3 multiply_reduce_fusion.13
  761.9 2.4 copy.418
  768.1 11.2 multiply_reduce_fusion
  779.4 12.4 multiply_convert_fusion.1
  791.9 2.9 multiply_convert_fusion.9
  797.8 4.7 fusion.50
  803.1 10.1 fusion.33
  813.3 12.7 while.27
  830.5 7.5 add_convert_fusion.1
  838.0 2.3 copy.433
  840.3 8.3 multiply_reduce_fusion.12
  852.1 28.2 %fusion.5 = (f32[1024]{0:T(1024)S(1)}, f32[1024]{0:T(1024)S(1)}, f32[1024]{0:T(1024)S(1)}, f32[1024]{0:T(1024)S(1)}, f32[2,1024,1024]{2,1,0:T(8,128)}, /*index=5...) fusion(f32[2,1027,1024]{2,1,0:T(8,128)} %copy-done.2, pred[2,1024]{1,0:T(4,128)(4,1)S(1)} %copy-done.73, ...), kind=kOutput, calls=%fused_computation.24 | convolution fusion | flops 3255824384 | bytes 71866368 | tf_op jit(solution)/shard_map/btkc,dkc->btd/dot_general | solution.py:327
  883.2 17.5 %pad_add_fusion = f32[2,1027,1024]{2,1,0:T(8,128)} fusion(f32[2,1024,1024]{2,1,0:T(8,128)} %get-tuple-element.249, f32[2,1024,1024]{2,1,0:T(8,128)} %get-tuple-element.248, f32[2,1024,1024]{2,1,0:T(8,128)} %get-tuple-element.247, f32[2,1024,1024]{2,1,0:T(8,128)} %get-tuple-element.250), kind=kLoop, calls=%fused_computation.15 | loop fusion | flops 6309888 | bytes 41967616 | tf_op jit(solution)/shard_map/add | solution.py:351
  900.9 10.4 multiply_reduce_fusion.4
  911.2 6.3 subtract_multiply_fusion
  917.7 9.7 fusion.69
  927.5 12.7 fusion.30
  941.4 4.5 convolution_bitcast_fusion
  945.9 7.9 fusion.66
  955.1 2.9 multiply_reduce_fusion.11
  958.0 2.8 multiply_reduce_fusion.10
  960.9 4.4 multiply_reduce_fusion.9
  965.2 2.7 pad_maximum_fusion.14
  968.6 24.1 %all-reduce.5 = f32[32,256]{1,0:T(8,128)S(1)} all-reduce(f32[32,256]{1,0:T(8,128)S(1)} %pad_maximum_fusion.11), channel_id=12, replica_groups=mesh['seq'=8,'head'=4] {'seq'}, use_global_device_ids=true, to_apply=%region_32.33.clone | all-reduce | flops 8192 | bytes 65536
  993.3 42.4 %all-reduce.6 = (f32[2,1024]{1,0:T(2,128)}, f32[4,1024]{1,0:T(4,128)}, f32[4]{0:T(128)S(1)}) all-reduce(f32[2,1024]{1,0:T(2,128)S(1)} %pad_maximum_fusion.13, f32[4,1024]{1,0:T(4,128)S(1)} %pad_maximum_fusion.12, f32[4]{0:T(128)S(1)} %pad_maximum_fusion.14), channel_id=1, replica_groups=mesh['seq'=8,'head'=4] {'seq','head'}, use_global_device_ids=true, to_apply=%region_35.36 | all-reduce | flops 6148 | bytes 49184 | tf_op jit(solution)/shard_map/psum | solution.py:381
  1036.2 2.3 copy.443
  1038.6 22.0 %reduce-scatter.13.cloned.1.call-done = f32[2,1024,256]{2,1,0:T(8,128)} async-done(((f32[2,1024,1024]{2,1,0:T(8,128)}), f32[2,1024,256]{2,1,0:T(8,128)}) %reduce-scatter.13.cloned.1.call-update) | async-done | bytes 2097168 | tf_op jit(solution)/shard_map/reduce_scatter | solution.py:363
  1060.6 4.6 fusion.93
  1065.1 45.1 %reduce-scatter.23.cloned.1.call-done = f32[704,128]{1,0:T(8,128)} async-done(((f32[704,1024]{1,0:T(8,128)}), f32[704,128]{1,0:T(8,128)}) %reduce-scatter.23.cloned.1.call-update) | async-done | bytes 360464 | tf_op jit(solution)/shard_map/reduce_scatter | solution.py:370
  1110.3 63.3 %reduce-scatter.21.cloned.1.call-done = f32[128,2,704]{0,2,1:T(8,128)} async-done(((f32[1024,2,704]{0,2,1:T(8,128)}), f32[128,2,704]{0,2,1:T(8,128)}) %reduce-scatter.21.cloned.1.call-update) | async-done | bytes 720912 | tf_op jit(solution)/shard_map/reduce_scatter | solution.py:369
  1173.6 39.8 %reduce-scatter.19.cloned.1.call-done = f32[256,128]{1,0:T(8,128)} async-done(((f32[256,1024]{1,0:T(8,128)}), f32[256,128]{1,0:T(8,128)}) %reduce-scatter.19.cloned.1.call-update) | async-done | bytes 131088 | tf_op jit(solution)/shard_map/reduce_scatter | solution.py:368
  1213.4 50.1 %reduce-scatter.17.cloned.1.call-done = f32[128,3,256]{2,0,1:T(8,128)} async-done(((f32[1024,3,256]{2,0,1:T(8,128)}), f32[128,3,256]{2,0,1:T(8,128)}) %reduce-scatter.17.cloned.1.call-update) | async-done | bytes 393232 | tf_op jit(solution)/shard_map/reduce_scatter | solution.py:367
  (327 shorter events, 72.8 us)
Async XLA Ops:
  7.2 435.9 %copy-start = (bf16[1024,2,704]{0,2,1:T(8,128)(2,1)S(1)}, bf16[1024,2,704]{0,2,1:T(8,128)(2,1)}, u32[]{:S(2)}) copy-start(bf16[1024,2,704]{0,2,1:T(8,128)(2,1)} %param.21) | copy-start | bytes 8650756
  7.2 108.4 %all-gather.8.cloned.1.call-start = ((), (), s32[]{:S(2)}) async-start(), calls=%async_computation.18 | async-start | bytes 2359296 | tf_op jit(solution)/shard_map/all_gather | solution.py:23
  11.5 468.2 %copy-start.76 = (f32[1,1024]{1,0:T(1,128)}, f32[1,1024]{1,0:T(1,128)S(1)}, u32[]{:S(2)}) copy-start(f32[1,1024]{1,0:T(1,128)S(1)} %get-tuple-element.276) | copy-start | bytes 12292
  13.1 10.4 copy-start.88
  13.1 10.4 copy-start.86
  16.0 46.5 %collective-permute-start = (bf16[2,3,1024]{2,1,0:T(4,128)(2,1)S(1)}, bf16[2,3,1024]{2,1,0:T(4,128)(2,1)S(1)}, u32[]{:S(2)}, u32[]{:S(2)}) collective-permute-start(bf16[2,3,1024]{2,1,0:T(4,128)(2,1)S(1)} %slice.143), channel_id=1, source_target_pairs={{0,4},{4,8},{8,12},{12,16},{16,20},{20,24},{24,28},{1,5},{5,9},{9,... | collective-permute-start | bytes 36872 | tf_op jit(solution)/shard_map/ppermute | solution.py:16
  23.6 40.2 %copy-start.78 = (f32[1,1024]{1,0:T(1,128)}, f32[1,1024]{1,0:T(1,128)S(1)}, u32[]{:S(2)}) copy-start(f32[1,1024]{1,0:T(1,128)S(1)} %get-tuple-element.269) | copy-start | bytes 12292
  23.6 40.2 %copy-start.80 = (f32[1,1024]{1,0:T(1,128)}, f32[1,1024]{1,0:T(1,128)S(1)}, u32[]{:S(2)}) copy-start(f32[1,1024]{1,0:T(1,128)S(1)} %get-tuple-element.270) | copy-start | bytes 12292
  23.6 40.2 %copy-start.82 = (f32[1,1024]{1,0:T(1,128)}, f32[1,1024]{1,0:T(1,128)S(1)}, u32[]{:S(2)}) copy-start(f32[1,1024]{1,0:T(1,128)S(1)} %get-tuple-element.271) | copy-start | bytes 12292
  23.6 40.2 %copy-start.84 = (f32[1,1024]{1,0:T(1,128)}, f32[1,1024]{1,0:T(1,128)S(1)}, u32[]{:S(2)}) copy-start(f32[1,1024]{1,0:T(1,128)S(1)} %get-tuple-element.272) | copy-start | bytes 12292
  49.2 14.6 %copy-start.70 = (pred[2,1024]{1,0:T(4,128)(4,1)}, pred[2,1024]{1,0:T(4,128)(4,1)S(1)}, u32[]{:S(2)}) copy-start(pred[2,1024]{1,0:T(4,128)(4,1)S(1)} %get-tuple-element.273) | copy-start | bytes 6148
  49.2 14.6 %copy-start.72 = (pred[2,1024]{1,0:T(4,128)(4,1)}, pred[2,1024]{1,0:T(4,128)(4,1)S(1)}, u32[]{:S(2)}) copy-start(pred[2,1024]{1,0:T(4,128)(4,1)S(1)} %get-tuple-element.274) | copy-start | bytes 6148
  49.3 14.6 %copy-start.74 = (pred[2,1024]{1,0:T(4,128)(4,1)}, pred[2,1024]{1,0:T(4,128)(4,1)S(1)}, u32[]{:S(2)}) copy-start(pred[2,1024]{1,0:T(4,128)(4,1)S(1)} %get-tuple-element.275) | copy-start | bytes 6148
  50.9 26.3 %copy-start.56 = (f32[2,2,1024]{2,1,0:T(2,128)}, f32[2,2,1024]{2,1,0:T(2,128)S(1)}, u32[]{:S(2)}) copy-start(f32[2,2,1024]{2,1,0:T(2,128)S(1)} %get-tuple-element.268) | copy-start | bytes 49156
  50.9 11.7 copy-start.19
  80.1 353.0 %all-reduce.9.cloned.1.call-start = ((), (), s32[]{:S(2)}) async-start(), calls=%async_computation.8 | async-start | bytes 16777216 | tf_op jit(solution)/shard_map/psum | solution.py:197
  104.0 9.0 copy-start.29
  115.7 13.1 %copy-start.63 = (f32[8,2,2]{2,1,0:T(2,128)}, f32[8,2,2]{2,1,0:T(2,128)S(1)}, u32[]{:S(2)}) copy-start(f32[8,2,2]{2,1,0:T(2,128)S(1)} %get-tuple-element.456) | copy-start | bytes 388
  120.0 8.8 copy-start.34
  120.0 9.8 copy-start.53
  134.3 493.1 %reduce-scatter.11.cloned.1.call-start = ((), (), s32[]{:S(2)}) async-start(), calls=%async_computation.10 | async-start | bytes 10485760 | tf_op jit(solution)/shard_map/reduce_scatter | solution.py:228
  443.0 36.6 %copy-start.66 = (f32[2,1024]{1,0:T(2,128)}, f32[2,1024]{1,0:T(2,128)S(1)}, u32[]{:S(2)}) copy-start(f32[2,1024]{1,0:T(2,128)S(1)} %add_rsqrt_fusion.2) | copy-start | bytes 24580
  443.0 12.9 %copy-start.93 = (bf16[704,1024]{1,0:T(8,128)(2,1)S(1)}, bf16[704,1024]{1,0:T(8,128)(2,1)}, u32[]{:S(2)}) copy-start(bf16[704,1024]{1,0:T(8,128)(2,1)} %param.22) | copy-start | bytes 4325380
  443.1 25.5 %slice-start.2 = ((s8[8388608]{0:T(1024)(128)(4,1)}), s8[4194304]{0:T(1024)(128)(4,1)S(1)}, s32[]{:S(2)}) async-start(s8[8388608]{0:T(1024)(128)(4,1)} %bitcast.390), calls=%async_computation.22 | async-start | bytes 8388608
  455.9 12.6 slice-start.3
  483.8 228.6 %copy-start.54 = (bf16[256,1024]{1,0:T(8,128)(2,1)S(1)}, bf16[256,1024]{1,0:T(8,128)(2,1)}, u32[]{:S(2)}) copy-start(bf16[256,1024]{1,0:T(8,128)(2,1)} %param.20) | copy-start | bytes 1572868
  483.8 228.5 %all-gather.6.cloned.1.call-start = ((), (), s32[]{:S(2)}) async-start(), calls=%async_computation.11 | async-start | bytes 5242880 | tf_op jit(solution)/shard_map/all_gather | solution.py:230
  630.9 88.3 %copy-start.24 = (bf16[2,2,1024,128]{2,3,1,0:T(8,128)(2,1)S(1)}, bf16[2,2,1024,128]{2,3,1,0:T(8,128)(2,1)}, u32[]{:S(2)}) copy-start(bf16[2,2,1024,128]{2,3,1,0:T(8,128)(2,1)} %get-tuple-element.297) | copy-start | bytes 3145732
  630.9 182.4 %all-gather.10.cloned.1.call-start = ((), (), s32[]{:S(2)}) async-start(), calls=%async_computation.19 | async-start | bytes 2359296 | tf_op jit(solution)/shard_map/all_gather | solution.py:23
  715.8 13.1 %copy-start.8 = (bf16[2,1024,256]{1,2,0:T(8,128)(2,1)}, bf16[2,1024,256]{1,2,0:T(8,128)(2,1)S(1)}, u32[]{:S(2)}) copy-start(bf16[2,1024,256]{1,2,0:T(8,128)(2,1)S(1)} %convolution_convert_fusion.1) | copy-start | bytes 3145732
  721.1 239.8 %reduce-scatter.9.cloned.1.call-start = ((), (), s32[]{:S(2)}) async-start(), calls=%async_computation.9 | async-start | bytes 5242880 | tf_op jit(solution)/shard_map/reduce_scatter | solution.py:209
  728.9 307.3 %reduce-scatter.15.cloned.1.call-start = ((), (), s32[]{:S(2)}) async-start(), calls=%async_computation.13 | async-start | bytes 4718592 | tf_op jit(solution)/shard_map/reduce_scatter | solution.py:366
  740.8 10.2 copy-start.7
  779.4 12.4 copy-start.33
  803.1 10.1 copy-start.51
  813.1 12.9 %copy-start.31 = (bf16[2,1024,1,256]{1,3,2,0:T(8,128)(2,1)S(1)}, bf16[2,1024,1,256]{1,3,2,0:T(8,128)(2,1)}, u32[]{:S(2)}) copy-start(bf16[2,1024,1,256]{1,3,2,0:T(8,128)(2,1)} %copy-done.28) | copy-start | bytes 3145732
  813.2 15.1 %copy-start.22 = (bf16[2,2,1024,128]{2,3,1,0:T(8,128)(2,1)S(1)}, bf16[2,2,1024,128]{2,3,1,0:T(8,128)(2,1)}, u32[]{:S(2)}) copy-start(bf16[2,2,1024,128]{2,3,1,0:T(8,128)(2,1)} %copy-done.20) | copy-start | bytes 3145732
  813.2 15.1 %copy-start.57 = (f32[2,2,1024]{2,1,0:T(2,128)S(1)}, f32[2,2,1024]{2,1,0:T(2,128)}, u32[]{:S(2)}) copy-start(f32[2,2,1024]{2,1,0:T(2,128)} %copy-done.56) | copy-start | bytes 49156
  813.2 247.4 %reduce-scatter.13.cloned.1.call-start = ((), (), s32[]{:S(2)}) async-start(), calls=%async_computation.12 | async-start | bytes 10485760 | tf_op jit(solution)/shard_map/reduce_scatter | solution.py:363
  830.4 9.9 copy-start.5
  830.4 9.9 copy-start.59
  840.3 8.4 copy-start.62
  852.1 28.2 %copy-start.52 = (bf16[2,1024,1,256]{3,1,2,0:T(8,128)(2,1)}, bf16[2,1024,1,256]{3,1,2,0:T(8,128)(2,1)S(1)}, u32[]{:S(2)}) copy-start(bf16[2,1024,1,256]{3,1,2,0:T(8,128)(2,1)S(1)} %copy.432) | copy-start | bytes 3145732
  880.3 20.4 %slice-start = ((s8[8388608]{0:T(1024)(128)(4,1)}), s8[4194304]{0:T(1024)(128)(4,1)S(1)}, s32[]{:S(2)}) async-start(s8[8388608]{0:T(1024)(128)(4,1)} %bitcast.380), calls=%async_computation.20 | async-start | bytes 8388608
  881.4 19.4 %slice-start.1 = ((s8[8388608]{0:T(1024)(128)(4,1)}), s8[4194304]{0:T(1024)(128)(4,1)S(1)}, s32[]{:S(2)}) async-start(s8[8388608]{0:T(1024)(128)(4,1)} %bitcast.380), calls=%async_computation.21 | async-start | bytes 8388608
  881.4 19.4 %copy-start.42 = (bf16[1024,4,256]{2,1,0:T(4,128)(2,1)S(1)}, bf16[1024,4,256]{2,1,0:T(4,128)(2,1)}, u32[]{:S(2)}) copy-start(bf16[1024,4,256]{2,1,0:T(4,128)(2,1)} %param.18) | copy-start | bytes 6291460
  881.5 19.4 %copy-start.48 = (bf16[2,1024,1,256]{3,1,2,0:T(8,128)(2,1)S(1)}, bf16[2,1024,1,256]{3,1,2,0:T(8,128)(2,1)}, u32[]{:S(2)}) copy-start(bf16[2,1024,1,256]{3,1,2,0:T(8,128)(2,1)} %copy.418) | copy-start | bytes 3145732
  881.5 19.4 %copy-start.49 = (bf16[2,1024,1,256]{3,1,2,0:T(8,128)(2,1)S(1)}, bf16[2,1024,1,256]{3,1,2,0:T(8,128)(2,1)}, u32[]{:S(2)}) copy-start(bf16[2,1024,1,256]{3,1,2,0:T(8,128)(2,1)} %copy.417) | copy-start | bytes 3145732
  881.5 19.4 %copy-start.50 = (bf16[2,1024,1,256]{3,1,2,0:T(8,128)(2,1)S(1)}, bf16[2,1024,1,256]{3,1,2,0:T(8,128)(2,1)}, u32[]{:S(2)}) copy-start(bf16[2,1024,1,256]{3,1,2,0:T(8,128)(2,1)} %copy.416) | copy-start | bytes 3145732
  881.5 19.4 %copy-start.61 = (f32[2,1024]{1,0:T(2,128)S(1)}, f32[2,1024]{1,0:T(2,128)}, u32[]{:S(2)}) copy-start(f32[2,1024]{1,0:T(2,128)} %copy-done.60) | copy-start | bytes 24580
  881.5 19.4 %copy-start.65 = (f32[1,1024]{1,0:T(1,128)S(1)}, f32[1,1024]{1,0:T(1,128)}, u32[]{:S(2)}) copy-start(f32[1,1024]{1,0:T(1,128)} %copy-done.64) | copy-start | bytes 12292
  881.5 19.3 %collective-permute-start.1 = (f32[2,3,1024]{2,1,0:T(4,128)S(1)}, f32[2,3,1024]{2,1,0:T(4,128)S(1)}, u32[]{:S(2)}, u32[]{:S(2)}) collective-permute-start(f32[2,3,1024]{2,1,0:T(4,128)S(1)} %pad_add_fusion.1), channel_id=1, source_target_pairs={{4,0},{8,4},{12,8},{16,12},{20,16},{24,20},{28,24},{5,1},{9,5},{13... | collective-permute-start | bytes 73736 | tf_op jit(solution)/shard_map/ppermute | solution.py:16
  917.6 9.8 copy-start.67
  917.6 9.8 copy-start.77
  917.6 192.6 %reduce-scatter.23.cloned.1.call-start = ((), (), s32[]{:S(2)}) async-start(), calls=%async_computation.17 | async-start | bytes 3244032 | tf_op jit(solution)/shard_map/reduce_scatter | solution.py:370
  927.4 246.2 %reduce-scatter.21.cloned.1.call-start = ((), (), s32[]{:S(2)}) async-start(), calls=%async_computation.16 | async-start | bytes 6488064 | tf_op jit(solution)/shard_map/reduce_scatter | solution.py:369
  940.2 273.2 %reduce-scatter.19.cloned.1.call-start = ((), (), s32[]{:S(2)}) async-start(), calls=%async_computation.15 | async-start | bytes 1179648 | tf_op jit(solution)/shard_map/reduce_scatter | solution.py:368
  945.9 317.6 %reduce-scatter.17.cloned.1.call-start = ((), (), s32[]{:S(2)}) async-start(), calls=%async_computation.14 | async-start | bytes 3538944 | tf_op jit(solution)/shard_map/reduce_scatter | solution.py:367
  955.1 12.8 %copy-start.11 = (bf16[2,1024,256]{1,2,0:T(8,128)(2,1)S(1)}, bf16[2,1024,256]{1,2,0:T(8,128)(2,1)}, u32[]{:S(2)}) copy-start(bf16[2,1024,256]{1,2,0:T(8,128)(2,1)} %copy-done.8) | copy-start | bytes 3145732
  955.1 12.8 %copy-start.55 = (bf16[2,2,1024,16]{2,3,0,1:T(8,128)(2,1)S(1)}, bf16[2,2,1024,16]{2,3,0,1:T(8,128)(2,1)}, u32[]{:S(2)}) copy-start(bf16[2,2,1024,16]{2,3,0,1:T(8,128)(2,1)} %get-tuple-element.257) | copy-start | bytes 393220
  958.0 10.3 copy-start.38
  958.0 10.3 copy-start.44
  960.9 32.4 %copy-start.91 = (f32[1024]{0:T(1024)S(1)}, f32[1024]{0:T(1024)}, u32[]{:S(2)}) copy-start(f32[1024]{0:T(1024)} %get-tuple-element.213) | copy-start | bytes 12292
  1036.2 227.2 %copy-start.1 = (bf16[1024,2,704]{0,2,1:T(8,128)(2,1)S(1)}, bf16[1024,2,704]{0,2,1:T(8,128)(2,1)}, u32[]{:S(2)}) copy-start(bf16[1024,2,704]{0,2,1:T(8,128)(2,1)} %param.21) | copy-start | bytes 8650756
  (49 other events, 196.7 us)
Sparse Core Ops, SparseCore 0:
  80.2 30.4 all-gather.7
  134.5 298.5 all-reduce.8
  483.9 143.4 reduce-scatter.10
  631.0 81.2 all-gather.5
  721.2 26.0 all-gather.9
  749.5 76.7 reduce-scatter.8
  830.0 51.8 reduce-scatter.14
  917.7 142.7 reduce-scatter.12
  1064.5 45.6 reduce-scatter.22
  1114.5 59.0 reduce-scatter.20
  1177.3 35.9 reduce-scatter.18
  1217.2 46.2 reduce-scatter.16
where the time goes:
time: 1270 us
  waiting for transfers between devices  744 us (59%)
  matrix products  258 us (20%)
  other arithmetic  124 us (10%)
  blocking collectives  76.4 us (6%)
  local copies, waits for them, and re-layouts  46 us (4%)
  between operations  16.6 us (1%)
    psum x1, waiting for transfers between devices, local(): mixed_out = lax.psum(mixed_part, 'head')  299 us
    reduce_scatter x1, waiting for transfers between devices, local(): lax.psum_scatter(grad_norm_terms, 'head', scatter_dimension=2, tiled=True)  144 us
    all_gather x1, waiting for transfers between devices, local(): lax.all_gather(grad_mid_share.astype(jnp.bfloat16), 'head', axis=2, tiled...  80.9 us
    reduce_scatter x1, waiting for transfers between devices, local(): lax.psum_scatter(grad_ffn_in, 'seq', scatter_dimension=0, tiled=True)  63.3 us
    reduce_scatter x1, waiting for transfers between devices, local(): lax.psum_scatter(grad_memory_in, 'seq', scatter_dimension=0, tiled=True)  50.1 us
    reduce_scatter x1, waiting for transfers between devices, local(): lax.psum_scatter(grad_ffn_out, 'seq', scatter_dimension=1, tiled=True)  45.1 us
    psum x1, blocking collectives, local(): lax.psum((jnp.stack([grad_gain_one, grad_gain_two]), grad_conv, squares),...  42.4 us
    reduce_scatter x1, waiting for transfers between devices, local(): lax.psum_scatter(grad_mixer_out, 'seq', scatter_dimension=1, tiled=True)  39.8 us
  transfers between devices with their start and end apart: 14, of which 8 were waited for; matrix products, arithmetic and copies ran while one was open for 25% of the time, Pallas kernels for 0%

commit v1 on v0

v1 whole, which is shorter than its diff:
```python
import jax
import jax.numpy as jnp
from jax import lax
from jax.sharding import PartitionSpec as P

HD = 128
EPS = 1e-06
F32 = jnp.float32
BF16 = jnp.bfloat16


def doc_index(doc_starts, positions):
    return jnp.sum((doc_starts[:, None, :] <= positions[None, :, None]).astype(jnp.int32), axis=-1)


def dot(a, b, dims):
    return lax.dot_general(a, b, (dims, ((), ())), preferred_element_type=F32)


class Place:
    def __init__(self, batches):
        self.ns = lax.axis_size("seq")
        self.nz = lax.axis_size("head")
        self.nl = self.nz // batches
        self.seq = lax.axis_index("seq")
        self.z = lax.axis_index("head")
        self.p = self.z // self.nl
        self.l = self.z % self.nl
        self.bits = [1 << i for i in range(self.ns.bit_length() - 1)]

    def across(self, value, bit):
        return lax.ppermute(value, "seq", [(i, i ^ bit) for i in range(self.ns)])

    def along(self, value, steps):
        first, last = max(0, -steps), min(self.ns, self.ns - steps)
        return lax.ppermute(value, "seq", [(i, i + steps) for i in range(first, last)])

    def other(self, value):
        return lax.ppermute(value, "head", [(i, (i + self.nl) % self.nz) for i in range(self.nz)])

    def group(self, value, steps):
        nl = self.nl
        return lax.ppermute(
            value,
            "head",
            [(i, i // nl * nl + (i % nl + steps) % nl) for i in range(self.nz)],
        )

    def bit_of(self, bit):
        return (self.seq // bit) % 2

    def fetch(self, weight, order):
        rows = weight.shape[0] // self.ns
        part = self.other(lax.dynamic_slice_in_dim(weight, self.seq * rows, rows, 0))
        done = []
        part = part[None]
        for bit in order:
            got = self.across(part, bit)
            mine = self.bit_of(bit) == 0
            pair = (jnp.where(mine, part, got), jnp.where(mine, got, part))
            done = sorted(done + [bit], reverse=True)
            axis = done.index(bit)
            lead = (2,) * axis
            split = (2,) * (len(done) - 1)
            tail = part.shape[1:]
            pair = [jnp.reshape(a, split + tail) for a in pair]
            part = jnp.stack(pair, axis=axis).reshape((-1,) + tail)
        return part.reshape(weight.shape)

    def scatter(self, grad, order):
        rows, cols = grad.shape
        left = list(reversed(self.bits))
        cur = grad.reshape((2,) * len(left) + (rows // self.ns, cols))
        for bit in order:
            axis = left.index(bit)
            mine = self.bit_of(bit)
            keep = lax.dynamic_index_in_dim(cur, mine, axis, False)
            send = lax.dynamic_index_in_dim(cur, 1 - mine, axis, False)
            got = self.across(send.astype(BF16), bit)
            cur = keep.astype(F32) + got.astype(F32)
            left.remove(bit)
        return cur

    def everywhere(self, value):
        for bit in self.bits:
            value = value + self.across(value, bit)
        return value

    def all_heads(self, value):
        total = value
        for steps in range(1, self.nz):
            total = total + lax.ppermute(
                value, "head", [(i, (i + steps) % self.nz) for i in range(self.nz)]
            )
        return total

    def scan(self, decay, state, reverse):
        pre_d, pre_s = jnp.ones_like(decay), jnp.zeros_like(state)
        tot_d, tot_s = decay, state
        for bit in self.bits:
            got_d, got_s = self.across(tot_d, bit), self.across(tot_s, bit)
            high = (self.bit_of(bit) == 1) ^ reverse
            new_pre_d = jnp.where(high, got_d * pre_d, pre_d)
            new_pre_s = jnp.where(high, pre_d[:, None, None] * got_s + pre_s, pre_s)
            early_d, early_s = jnp.where(high, got_d, tot_d), jnp.where(high, got_s, tot_s)
            late_d, late_s = jnp.where(high, tot_d, got_d), jnp.where(high, tot_s, got_s)
            tot_d = early_d * late_d
            tot_s = late_d[:, None, None] * early_s + late_s
            pre_d, pre_s = new_pre_d, new_pre_s
        return pre_s


def heads_of(values, count):
    return jnp.transpose(values.reshape(values.shape[0], count, HD), (1, 0, 2))


def flat_of(values):
    return jnp.transpose(values, (1, 0, 2)).reshape(values.shape[1], -1)


def unit_back(raw_rows, inv_len, grad_rows):
    unit_vals = raw_rows * inv_len
    return inv_len * (
        grad_rows - unit_vals * jnp.sum(unit_vals * grad_rows, axis=-1, keepdims=True)
    )


def norm_back(values, inv_len, gain_row, grad_rows):
    hat_rows = values * inv_len
    scaled = grad_rows * gain_row
    grad_values = inv_len * (
        scaled - hat_rows * jnp.mean(scaled * hat_rows, axis=-1, keepdims=True)
    )
    return (grad_values, jnp.sum(grad_rows * hat_rows, axis=0))


def local(
    stream,
    cotangent,
    mixer_in,
    memory_in,
    mixer_out,
    ffn_in,
    ffn_out,
    persistent,
    norm_gains,
    conv_weight,
    decays,
    doc_starts,
):
    batches, seg_len, width = stream.shape
    at = Place(batches)
    own_heads = mixer_out.shape[0] // HD
    heads = 2 * own_heads
    own_cols = own_heads * HD
    own_hidden = ffn_out.shape[0]
    taps = conv_weight.shape[0]
    rim = taps - 1
    persist = persistent.shape[0] // 2
    scale = HD**-0.5
    high_bits = list(reversed(at.bits[1:]))
    order_a = high_bits + at.bits[:1]
    order_b = at.bits[1:] + at.bits[:1]
    back_a = at.bits[:1] + high_bits
    back_b = at.bits[:1] + at.bits[1:]

    mixer_two = jnp.concatenate(
        [mixer_in.reshape(width, -1), at.fetch(mixer_in.reshape(width, -1), order_a)], axis=1
    ).reshape(width, 2, 4, own_cols)
    memory_two = jnp.concatenate(
        [memory_in.reshape(width, -1), at.fetch(memory_in.reshape(width, -1), order_b)], axis=1
    ).reshape(width, 2, 3, own_cols)
    out_two = jnp.concatenate([mixer_out, at.fetch(mixer_out, order_b)], axis=0)
    ffn_in_two = jnp.concatenate([ffn_in, at.fetch(ffn_in.reshape(width, -1), order_a).reshape(ffn_in.shape)], axis=2)
    ffn_out_two = jnp.concatenate([ffn_out, at.fetch(ffn_out, order_b)], axis=0)
    persist_two = jnp.concatenate([persistent, at.other(persistent)], axis=1)
    pick = lambda a: lax.dynamic_index_in_dim(a, at.p, 0, False)
    drop = lambda a: lax.dynamic_index_in_dim(a, 1 - at.p, 0, False)
    decay_two = jnp.concatenate([pick(decays), at.other(drop(decays))], axis=0)
    rows_in = pick(stream)
    cot = pick(cotangent)
    starts = lax.dynamic_slice_in_dim(doc_starts, at.p, 1, 0)

    first_pos = at.seq * seg_len
    positions = first_pos + jnp.arange(seg_len, dtype=jnp.int32)
    doc_ids = doc_index(starts, positions)[0]
    rim_ids = doc_index(starts, first_pos - rim + jnp.arange(rim, dtype=jnp.int32))[0]
    prev_id = doc_index(starts, jnp.reshape(first_pos - 1, (1,)))[0]
    end_id = doc_ids[seg_len - 1 :]
    allowed = (positions[:, None] >= positions[None, :]) & (doc_ids[:, None] == doc_ids[None, :])

    inv_one = lax.rsqrt(jnp.mean(rows_in * rows_in, axis=-1, keepdims=True) + EPS)
    normed = (rows_in * inv_one * norm_gains[0]).astype(BF16)
    rim_rows = at.along(normed[seg_len - rim :], 1)
    extended = jnp.concatenate([rim_rows, normed], axis=0).astype(F32)
    ext_ids = jnp.concatenate([rim_ids, doc_ids], axis=0)
    tap_masks = []
    conv_sum = jnp.zeros(rows_in.shape, F32)
    for tap in range(taps):
        lead = rim - tap
        same = (ext_ids[lead : lead + seg_len] == doc_ids)[:, None]
        tap_masks.append(same)
        conv_sum = conv_sum + jnp.where(same, extended[lead : lead + seg_len], 0.0) * conv_weight[tap]
    conv_out = conv_sum.astype(BF16)

    def project(values, weight, count):
        full = dot(values, weight.reshape(width, -1), ((1,), (0,)))
        full = full.reshape(seg_len, 2, count, own_heads, HD)
        return [
            jnp.transpose(full[:, :, i].reshape(seg_len, heads, HD), (1, 0, 2)) for i in range(count)
        ]

    queries, keys, values, gate_pre_mix = project(normed, mixer_two, 4)
    queries, keys, values = queries.astype(BF16), keys.astype(BF16), values.astype(BF16)
    gate_open = jax.nn.sigmoid(gate_pre_mix)
    per_keys = heads_of(persist_two[:persist], heads)
    per_values = heads_of(persist_two[persist:], heads)

    def bdot(a, b, ca, cb):
        return lax.dot_general(a, b, (((ca,), (cb,)), ((0,), (0,))), preferred_element_type=F32)

    def scores():
        seg = jnp.where(allowed[None], scale * bdot(queries, keys, 2, 2), -1e30)
        per = scale * bdot(queries, per_keys, 2, 2)
        return seg, per

    seg_scores, per_scores = scores()
    row_top = jnp.maximum(jnp.max(seg_scores, -1), jnp.max(per_scores, -1))[..., None]
    seg_exp = jnp.exp(seg_scores - row_top)
    per_exp = jnp.exp(per_scores - row_top)
    row_total = jnp.sum(seg_exp, -1, keepdims=True) + jnp.sum(per_exp, -1, keepdims=True)
    log_total = row_top + jnp.log(row_total)
    attended = bdot((seg_exp / row_total).astype(BF16), values, 2, 1)
    attended = attended + bdot((per_exp / row_total).astype(BF16), per_values, 2, 1)

    query_raw, key_raw, value_raw = project(conv_out, memory_two, 3)
    query_inv = lax.rsqrt(jnp.sum(query_raw * query_raw, -1, keepdims=True) + EPS)
    key_inv = lax.rsqrt(jnp.sum(key_raw * key_raw, -1, keepdims=True) + EPS)
    mem_query = (query_raw * query_inv).astype(BF16)
    mem_key = (key_raw * key_inv).astype(BF16)
    mem_value = value_raw.astype(BF16)
    log_sums = jnp.cumsum(jnp.log(decay_two), axis=-1)
    gaps = log_sums[:, :, None] - log_sums[:, None, :]
    decay_grid = jnp.where(allowed[None], jnp.exp(jnp.minimum(gaps, 0.0)), 0.0)
    mem_weights = (bdot(mem_query, mem_key, 2, 2) * decay_grid).astype(BF16)
    recalled = bdot(mem_weights, mem_value, 2, 1)
    inflow = jnp.exp(log_sums) * (doc_ids == prev_id).astype(F32)[None]
    keep = jnp.exp(log_sums[:, seg_len - 1 :] - log_sums) * (doc_ids == end_id).astype(F32)[None]
    carry = jnp.exp(log_sums[:, seg_len - 1]) * (end_id == prev_id).astype(F32)
    kept_keys = (mem_key.astype(F32) * keep[..., None]).astype(BF16)
    state_in = at.scan(carry, bdot(kept_keys, mem_value, 1, 1), False)
    in_queries = (mem_query.astype(F32) * inflow[..., None]).astype(BF16)
    state_low = state_in.astype(BF16)
    recalled = recalled + bdot(in_queries, state_low, 2, 1)
    branch = (attended + gate_open * recalled).astype(BF16)
    flat_branch = flat_of(branch)

    def group_sum(part):
        total = part.astype(F32)
        for steps in range(1, at.nl):
            total = total + at.group(part, steps).astype(F32)
        return total

    mixed_out = group_sum(dot(flat_branch, out_two, ((1,), (0,))).astype(BF16))
    middle = rows_in + mixed_out
    inv_two = lax.rsqrt(jnp.mean(middle * middle, axis=-1, keepdims=True) + EPS)
    normed_two = (middle * inv_two * norm_gains[1]).astype(BF16)
    gate_pre = dot(normed_two, ffn_in_two[:, 0], ((1,), (0,)))
    up_part = dot(normed_two, ffn_in_two[:, 1], ((1,), (0,)))
    gate_sigmoid = jax.nn.sigmoid(gate_pre)
    silu_gate = gate_pre * gate_sigmoid
    hidden = (silu_gate * up_part).astype(BF16)
    ffn_part = dot(hidden, ffn_out_two, ((1,), (0,))).astype(BF16)

    col = width // at.nz

    def columns(value):
        return lax.dynamic_index_in_dim(value.reshape(seg_len, batches, at.nl, col), at.l, 2, False)

    def group_scatter(part):
        total = columns(part).astype(F32)
        view = part.reshape(seg_len, batches, at.nl, col)
        for steps in range(1, at.nl):
            send = lax.dynamic_index_in_dim(view, (at.l + steps) % at.nl, 2, False)
            total = total + at.group(send, steps).astype(F32)
        return total

    def placed(share):
        mine = lax.dynamic_index_in_dim(share, at.p, 1, False)
        got = at.other(lax.dynamic_index_in_dim(share, 1 - at.p, 1, False).astype(BF16)).astype(F32)
        return jnp.where(at.p == 0, jnp.stack([mine, got]), jnp.stack([got, mine]))

    ffn_share = group_scatter(ffn_part)
    result_share = columns(middle) + ffn_share
    result = placed(result_share)

    grad_ffn = cot.astype(BF16)
    grad_hidden = dot(grad_ffn, ffn_out_two, ((1,), (1,)))
    silu_slope = gate_sigmoid * (1.0 + gate_pre * (1.0 - gate_sigmoid))
    grad_gate_pre = (grad_hidden * up_part * silu_slope).astype(BF16)
    grad_up = (grad_hidden * silu_gate).astype(BF16)
    grad_normed_two = dot(grad_gate_pre, ffn_in_two[:, 0], ((1,), (1,))) + dot(
        grad_up, ffn_in_two[:, 1], ((1,), (1,))
    )
    grad_normed_two = group_sum(grad_normed_two.astype(BF16))

    def weight_grad(a, b, order):
        return at.scatter(dot(a, b, ((0,), (0,))).astype(BF16), order)

    h = own_hidden
    fg = weight_grad(normed_two, grad_gate_pre, back_a)
    fu = weight_grad(normed_two, grad_up, back_b)
    fo = weight_grad(grad_ffn, hidden, back_a)

    def both(mine, theirs):
        return mine + at.other(theirs.astype(BF16)).astype(F32)

    grad_ffn_in = jnp.stack([both(fg[:, :h], fg[:, h:]), both(fu[:, :h], fu[:, h:])], axis=1)
    grad_ffn_out = both(fo[:, :h], fo[:, h:]).T

    grad_norm, grad_gain_two = norm_back(middle, inv_two, norm_gains[1], grad_normed_two)
    grad_mid = grad_norm + cot
    grad_mix = grad_mid.astype(BF16)
    fm = weight_grad(grad_mix, flat_branch, back_b)
    grad_mixer_out = both(fm[:, :own_cols], fm[:, own_cols:]).T
    grad_flat = dot(grad_mix, out_two, ((1,), (1,))).astype(BF16)
    grad_branch = heads_of(grad_flat, heads)
    gb_wide = grad_branch.astype(F32)
    grad_recalled = (gb_wide * gate_open).astype(BF16)
    grad_gate_mix = (gb_wide * recalled * gate_open * (1.0 - gate_open)).astype(BF16)
    grad_state = at.scan(carry, bdot(in_queries, grad_recalled, 1, 1), True)
    gs_low = grad_state.astype(BF16)

    seg_scores, per_scores = scores()
    seg_probs = jnp.exp(seg_scores - log_total)
    per_probs = jnp.exp(per_scores - log_total)
    seg_gp = bdot(grad_branch, values, 2, 2)
    per_gp = bdot(grad_branch, per_values, 2, 2)
    delta = jnp.sum(seg_probs * seg_gp, -1, keepdims=True) + jnp.sum(per_probs * per_gp, -1, keepdims=True)
    seg_gs = (seg_probs * (seg_gp - delta)).astype(BF16)
    per_gs = (per_probs * (per_gp - delta)).astype(BF16)
    grad_queries = scale * (bdot(seg_gs, keys, 2, 1) + bdot(per_gs, per_keys, 2, 1))
    grad_keys = scale * bdot(seg_gs, queries, 1, 1)
    grad_per_keys = scale * bdot(per_gs, queries, 1, 1)
    grad_values = bdot(seg_probs.astype(BF16), grad_branch, 1, 1)
    grad_per_values = bdot(per_probs.astype(BF16), grad_branch, 1, 1)
    grad_persist = jnp.concatenate([flat_of(grad_per_keys), flat_of(grad_per_values)], axis=0)

    grad_ms = (bdot(grad_recalled, mem_value, 2, 2) * decay_grid).astype(BF16)
    grad_mq = bdot(grad_ms, mem_key, 2, 1) + inflow[..., None] * bdot(grad_recalled, state_low, 2, 2)
    grad_mk = bdot(grad_ms, mem_query, 1, 1) + keep[..., None] * bdot(mem_value, gs_low, 2, 2)
    grad_mv = bdot(mem_weights, grad_recalled, 1, 1) + bdot(kept_keys, gs_low, 2, 1)
    grad_qr = unit_back(query_raw, query_inv, grad_mq)
    grad_kr = unit_back(key_raw, key_inv, grad_mk)

    def cat(parts):
        stacked = [jnp.transpose(a.astype(BF16), (1, 0, 2)).reshape(seg_len, 2, own_cols) for a in parts]
        return jnp.stack(stacked, axis=2).reshape(seg_len, -1)

    mem_cat = cat([grad_qr, grad_kr, grad_mv])
    mix_cat = cat([grad_queries, grad_keys, grad_values, grad_gate_mix])
    mm = weight_grad(conv_out, mem_cat, back_a)
    half = mm.shape[1] // 2
    grad_memory_in = both(mm[:, :half], mm[:, half:]).reshape(-1, 3, own_cols)
    mi = weight_grad(normed, mix_cat, back_b)
    half = mi.shape[1] // 2
    grad_mixer_in = both(mi[:, :half], mi[:, half:]).reshape(-1, 4, own_cols)
    grad_conv_out = dot(mem_cat, memory_two.reshape(width, -1), ((1,), (1,)))
    grad_normed = dot(mix_cat, mixer_two.reshape(width, -1), ((1,), (1,)))
    grad_ext = jnp.zeros((seg_len + rim, width), F32)
    conv_terms = []
    for tap in range(taps):
        lead = rim - tap
        masked = jnp.where(tap_masks[tap], grad_conv_out, 0.0)
        conv_terms.append(jnp.sum(masked * extended[lead : lead + seg_len], axis=0))
        grad_ext = grad_ext + jnp.pad(masked * conv_weight[tap], ((lead, tap), (0, 0)))
    grad_conv = jnp.stack(conv_terms)
    rim_grads = at.along(grad_ext[:rim], -1)
    grad_normed = grad_normed + grad_ext[rim:] + jnp.pad(rim_grads, ((seg_len - rim, 0), (0, 0)))
    grad_in, grad_gain_one = norm_back(rows_in, inv_one, norm_gains[0], grad_normed)
    grad_stream = placed(group_scatter(grad_in.astype(BF16)) + columns(grad_mid))

    share = 1.0 / at.nl
    squares = jnp.stack(
        [
            jnp.sum(rows_in * rows_in) * share,
            jnp.sum(mixed_out * mixed_out) * share,
            jnp.sum(ffn_share * ffn_share),
            jnp.sum(result_share * result_share),
        ]
    )
    small = jnp.concatenate(
        [
            grad_gain_one[None],
            grad_gain_two[None] * share,
            grad_conv,
            jnp.pad(squares, (0, width - 4))[None],
        ],
        axis=0,
    )
    small = at.all_heads(at.everywhere(small))
    rows_p = persistent.shape[0] // at.ns
    gp = at.everywhere(grad_persist)
    gp = lax.dynamic_slice_in_dim(gp, at.seq * rows_p, rows_p, 0)
    grad_persistent = gp[:, :own_cols] + at.other(gp[:, own_cols:])
    cells = float(batches * seg_len * at.ns * width)
    rms_values = jnp.sqrt(small[2 + taps, :4] / cells)
    return (
        result,
        grad_stream,
        grad_mixer_in,
        grad_memory_in,
        grad_mixer_out,
        grad_ffn_in,
        grad_ffn_out,
        grad_persistent,
        small[:2],
        small[2 : 2 + taps],
        rms_values,
    )


def solution(mesh):
    placed = (
        P(None, "seq", None),
        P(None, "seq", None),
        P(None, None, "head"),
        P(None, None, "head"),
        P("head", None),
        P(None, None, "head"),
        P("head", None),
        P(None, "head"),
        P(),
        P(),
        P(None, "head", "seq"),
        P(),
    )
    return jax.shard_map(
        local,
        mesh=mesh,
        in_specs=placed,
        out_specs=(
            P(None, "seq", "head"),
            P(None, "seq", "head"),
            P("seq", None, "head"),
            P("seq", None, "head"),
            P("head", "seq"),
            P("seq", None, "head"),
            P("head", "seq"),
            P("seq", "head"),
            P(),
            P(),
            P(),
        ),
        check_vma=False,
    )
```

time: 1270 us -> 790 us (0.62)
  waiting for transfers between devices: 744 us -> 166 us
  local copies, waits for them, and re-layouts: 46 us -> 180 us
  starting transfers between devices: 5.43 us -> 84.6 us
  blocking collectives: 76.4 us -> 0 us
  matrix products: 258 us -> 208 us
    reduce_scatter x8 -> x0, waiting for transfers between devices: 364 us -> none  [the longest x1 144 us: local(): lax.psum_scatter(grad_norm_terms, 'head', scatter_dimension=2, tiled=True)]
    psum x1 -> x0, waiting for transfers between devices: 299 us -> none  [local(): mixed_out = lax.psum(mixed_part, 'head')]
    ppermute x2 -> x73, waiting for transfers between devices: 0.01 us -> 166 us  [the longest x16 76.7 us: other(): lax.ppermute(value, 'head', [(i, (i + self.nl) % self.nz) for i in range(...]
    all_gather x3 -> x0, waiting for transfers between devices: 80.9 us -> none  [the longest x1 80.9 us: local(): lax.all_gather(grad_mid_share.astype(jnp.bfloat16), 'head', axis=2, tiled...]
    ppermute x2 -> x73, starting transfers between devices: 4.08 us -> 84.6 us  [the longest x48 47.6 us: across(): return lax.ppermute(value, 'seq', [(i, i ^ bit) for i in range(self.ns)])]
    dynamic_slice x0 -> x25, local copies, waits for them, and re-layouts: none -> 58.3 us  [the longest x4 20.1 us: local(): pick = lambda a: lax.dynamic_index_in_dim(a, at.p, 0, False)]
    dot_general x39 -> x42, matrix products: 258 us -> 208 us  [the longest x18 125 us: dot(): return lax.dot_general(a, b, (dims, ((), ())), preferred_element_type=F32)]
    psum x1 -> x0, blocking collectives: 42.4 us -> none  [local(): lax.psum((jnp.stack([grad_gain_one, grad_gain_two]), grad_conv, squares),...]
  transfers between devices with their start and end apart: 14 -> 73, of which waited for: 8 -> 30; matrix products, arithmetic and copies ran while one was open for 25% -> 58% of each run, Pallas kernels for 0% -> 0%
where the time goes in v1:
time: 790 us; the launch traced here: 778 us
  matrix products  208 us (26%)
  local copies, waits for them, and re-layouts  180 us (23%)
  waiting for transfers between devices  166 us (21%)
  other arithmetic  133 us (17%)
  starting transfers between devices  84.6 us (11%)
    dot_general x18, matrix products, dot(): return lax.dot_general(a, b, (dims, ((), ())), preferred_element_type=F32)  125 us
    dot_general x24, matrix products, bdot(): lax.dot_general(a, b, (((ca,), (cb,)), ((0,), (0,))), preferred_element_t...  83.8 us
    ppermute x16, waiting for transfers between devices, other(): lax.ppermute(value, 'head', [(i, (i + self.nl) % self.nz) for i in range(...  76.7 us
    ppermute x48, waiting for transfers between devices, across(): return lax.ppermute(value, 'seq', [(i, i ^ bit) for i in range(self.ns)])  61.6 us
    ppermute x48, starting transfers between devices, across(): return lax.ppermute(value, 'seq', [(i, i ^ bit) for i in range(self.ns)])  47.6 us
    unnamed x321, local copies, waits for them, and re-layouts  42.9 us
    ppermute x16, starting transfers between devices, other(): lax.ppermute(value, 'head', [(i, (i + self.nl) % self.nz) for i in range(...  25 us
    dynamic_slice x4, local copies, waits for them, and re-layouts, local(): pick = lambda a: lax.dynamic_index_in_dim(a, at.p, 0, False)  20.1 us
  transfers between devices with their start and end apart: 73, of which 30 were waited for; matrix products, arithmetic and copies ran while one was open for 58% of the time, Pallas kernels for 0%

profile of v1, /device:TPU:0, one launch (start us, length us, event | category | flops | bytes accessed | tf_op | source)
XLA Modules:
  0.0 778.3 jit_solution(7025252729974628564)
XLA Ops:
  0.7 4.7 constant_dynamic-slice_fusion.27
  5.4 5.4 copy.235
  35.6 4.7 constant_dynamic-slice_fusion.15
  50.3 5.3 copy.265
  61.3 5.6 add_convert_fusion.1
  80.9 9.7 %collective-permute-done.16 = bf16[32,1024]{1,0:T(8,128)(2,1)S(1)} collective-permute-done((bf16[32,1024]{1,0:T(8,128)(2,1)S(1)}, bf16[32,1024]{1,0:T(8,128)(2,1)S(1)}, u32[]{:S(2)}, u32[]{:S(2)}) %collective-permute-start.16) | collective-permute-done | bytes 65568 | tf_op jit(solution)/shard_map/ppermute | solution.py:39
  115.8 6.7 collective-permute-done.22
  125.0 4.1 collective-permute-done.8
  133.1 5.4 collective-permute-done.23
  146.1 4.0 reshape_reshape.13
  150.1 7.5 fusion.43
  157.6 8.2 %reshape.582 = f32[1024,2,3,2,128]{4,3,2,1,0:T(2,128)} reshape(f32[1024,1536]{1,0:T(8,128)} %fusion.43) | data formatting | bytes 12582912 | tf_op jit(solution)/shard_map/reshape | solution.py:208
  165.8 5.7 fusion.116
  184.9 3.7 copy.254
  191.2 7.2 multiply_convert_fusion.2
  210.7 6.4 copy.238
  217.1 11.4 %fusion.120 = (bf16[1024,2,4,2,128]{0,4,3,2,1:T(8,128)(2,1)S(1)}, f32[1024,2,4,2,128]{0,4,3,2,1:T(8,128)}) fusion(bf16[2,4,2,128,1024]{4,3,2,1,0:T(8,128)(2,1)} %bitcast.591, f32[1024]{0:T(1024)S(1)} %bitcast.649, f32[1,1024,1024]{2,1,0:T(8,128)} %constant_dynamic-slice_fusion.27, f32[1024]{0:T(1024)S(1)} %add_rsqrt_fusion.3), kind=kOutput, calls=%fused_computation.400 | convolution fusion | flops 4300210176 | bytes 20979712 | tf_op jit(solution)/shard_map/dot_general | solution.py:17
  234.3 7.4 fusion.121
  242.2 8.1 %fusion = f32[4,1024]{1,0:T(4,128)S(1)} fusion(f32[4,1024,1024]{1,2,0:T(8,128)} %get-tuple-element.157, f32[4,1024]{1,0:T(4,128)S(1)} %max.10), kind=kLoop, calls=%fused_computation.9 | loop fusion | flops 8384512 | bytes 16809984 | tf_op jit(solution)/shard_map/reduce_sum | solution.py:231
  251.0 7.6 fusion.5
  271.1 5.3 fusion.46
  279.9 8.0 %copy.262 = bf16[2,2,2,128,1408]{3,2,1,0,4:T(2,128)(2,1)} copy(bf16[2,2,2,128,1408]{4,3,1,0,2:T(8,128)(2,1)} %pad_maximum_fusion.4) | data formatting | bytes 5767168 | tf_op jit(solution)/shard_map/stack | solution.py:67
  288.0 7.4 reshape_reshape_reshape.3
  295.4 3.9 constant_dynamic-update-slice_fusion.2
  299.3 15.6 %collective-permute-done.20 = bf16[1024,1024]{0,1:T(8,128)(2,1)} collective-permute-done((bf16[1024,1024]{0,1:T(8,128)(2,1)}, bf16[1024,1024]{0,1:T(8,128)(2,1)}, u32[]{:S(2)}, u32[]{:S(2)}) %collective-permute-start.20) | collective-permute-done | bytes 2097184 | tf_op jit(solution)/shard_map/ppermute | solution.py:43
  314.9 4.1 multiply_reduce_fusion.10
  319.4 3.7 copy-done.77
  323.2 5.5 fusion.16
  328.6 9.9 %multiply_convert_fusion.3 = (bf16[1024,1408]{1,0:T(8,128)(2,1)}, bf16[1024,1408]{1,0:T(8,128)(2,1)}, bf16[1024,1408]{1,0:T(8,128)(2,1)}) fusion(f32[1024,1408]{1,0:T(8,128)S(1)} %bitcast.677, f32[1024,1408]{1,0:T(8,128)} %fusion.16, bf16[1024,1024]{0,1:T(8,128)(2,1)S(1)} %multiply_convert_fusion.7, bf16[1024,2,1408]{0,2,1:T(8,128)(2,1)S(1)} %copy-done.77), kind=kOutput, calls=%fused_computation.14 | convolution fusion | flops 2974416896 | bytes 25165824 | tf_op jit(solution)/shard_map/dot_general | solution.py:17
  338.5 5.6 fusion.13
  344.1 4.7 convolution_convert_fusion.1
  348.9 4.7 add_convert_fusion
  358.7 6.6 fusion.124
  372.6 5.8 convolution_convert_fusion.2
  390.8 7.5 convolution_convert_fusion.5
  410.5 3.9 multiply_reduce_fusion.6
  414.5 3.8 bitcast_add_fusion
  422.6 7.7 multiply_convert_fusion
  432.1 9.7 %fusion.47 = bf16[4,1024,128]{1,2,0:T(8,128)(2,1)} fusion(bf16[4,1024,128]{1,2,0:T(8,128)(2,1)S(1)} %bitcast.562, f32[4,1024,1024]{1,2,0:T(8,128)} %get-tuple-element.157, f32[4,1024]{1,0:T(4,128)S(1)} %copy-done.72), kind=kOutput, calls=%fused_computation.148 | convolution fusion | flops 1082654720 | bytes 18890752 | tf_op jit(solution)/shard_map/dot_general | solution.py:220
  441.8 8.5 %multiply_reduce_fusion = (f32[4,1024]{1,0:T(4,128)}, f32[4,1024,1024]{1,2,0:T(8,128)S(1)}) fusion(f32[4,1024,1024]{1,2,0:T(8,128)} %get-tuple-element.157, f32[4,1024]{1,0:T(4,128)} %get-tuple-element.55, bf16[4,1024,128]{1,2,0:T(8,128)(2,1)S(1)} %bitcast.563, bf16[4,1024,128]{1,2,0:T(8,128)(2,1)} %bitcast.584), kind=kOutput, calls=%fused_computation.2 | convolution fusion | flops 1086320640 | bytes 35684352 | tf_op jit(solution)/shard_map/dot_general | solution.py:220
  452.3 4.9 convolution_convert_fusion.8
  459.9 10.9 %multiply_convert_fusion.1 = bf16[4,1024,1024]{1,2,0:T(8,128)(2,1)} fusion(f32[4,1024,1024]{1,2,0:T(8,128)S(1)} %get-tuple-element.165, f32[4,1024,1024]{1,2,0:T(8,128)} %get-tuple-element.157, f32[4,1024]{1,0:T(4,128)S(1)} %add.553, f32[4,1024]{1,0:T(4,128)S(1)} %copy-done.73), kind=kLoop, calls=%fused_computation.1 | loop fusion | flops 16777216 | bytes 41975808 | tf_op jit(solution)/shard_map/convert_element_type | solution.py:340
  470.9 6.5 multiply_convert_fusion.10
  486.2 9.7 %convolution_convert_fusion.4 = bf16[1024,2048]{1,0:T(8,128)(2,1)} fusion(bf16[1024,2048]{0,1:T(8,128)(2,1)} %bitcast.589, f32[1,1024,1024]{2,1,0:T(8,128)S(1)} %copy-done.19, f32[1024]{0:T(1024)S(1)} %bitcast.650, f32[1024]{0:T(1024)S(1)} %copy-done.109), kind=kOutput, calls=%fused_computation.59 | convolution fusion | flops 4300210176 | bytes 12591104 | tf_op jit(solution)/shard_map/dot_general | solution.py:17
  503.3 4.2 fusion.128
  524.2 4.0 collective-permute-done.65
  538.2 5.9 collective-permute-done.53
  546.8 4.9 collective-permute-done.61
  560.7 5.2 collective-permute-done.54
  572.8 6.5 multiply_reduce_fusion.13
  582.6 13.5 %multiply_reduce_fusion.2 = (f32[1024]{0:T(1024)S(1)}, f32[1024]{0:T(1024)S(1)}, f32[1024]{0:T(1024)S(1)}, f32[1024]{0:T(1024)}, f32[1024,1024]{0,1:T(8,128)}, /...) fusion(f32[1027,1024]{0,1:T(8,128)S(1)} %bitcast.560, pred[1024]{0:T(1024)(128)(4,1)S(1)} %copy-done.132, ...), kind=kOutput, calls=%fused_computation.31 | convolution fusion | flops 3243241472 | bytes 39881728 | tf_op jit(solution)/shard_map/dot_general | solution.py:17
  600.6 10.6 %pad_add_fusion = f32[1027,1024]{0,1:T(8,128)} fusion(f32[1024,1024]{0,1:T(8,128)S(1)} %copy-done.22, f32[1024,1024]{0,1:T(8,128)} %get-tuple-element.73, f32[1024,1024]{0,1:T(8,128)} %get-tuple-element.74, f32[1024,1024]{0,1:T(8,128)} %get-tuple-element.76), kind=kLoop, calls=%fused_computation.19 | loop fusion | flops 3154944 | bytes 20983808 | tf_op jit(solution)/shard_map/add | solution.py:376
  613.1 10.1 %multiply_reduce_fusion.7 = (f32[1024]{0:T(1024)}, f32[1024]{0:T(1024)S(1)}, f32[]{:T(128)}, f32[1024,1024]{0,1:T(8,128)S(1)}) fusion(f32[1,1024,1024]{1,2,0:T(8,128)S(1)} %copy-done.2, f32[1024]{0:T(1024)S(1)} %copy-done.109, f32[1024]{0:T(1024)S(1)} %bitcast.651, f32[3,1024]{0,1:T(8,128)} %collective-permute-done.36, f32[1027,1024]{0,1:T(8,128)} %pad_add_fusion, ...), kind=kOutput, calls=%fused_computation.36 | convolution fusion | flops 4313839616 | bytes 21000196 | tf_op jit(solution)/shard_map/dot_general | solution.py:17
  627.9 7.7 convolution_convert_fusion.3
  649.5 25.6 %collective-permute-done.50 = bf16[128,256]{0,1:T(8,128)(2,1)S(1)} collective-permute-done((bf16[128,256]{0,1:T(8,128)(2,1)S(1)}, bf16[128,256]{0,1:T(8,128)(2,1)S(1)}, u32[]{:S(2)}, u32[]{:S(2)}) %collective-permute-start.50) | collective-permute-done | bytes 65568 | tf_op jit(solution)/shard_map/ppermute | solution.py:39
  675.8 4.8 multiply_reduce_fusion.11
  699.3 12.5 %collective-permute-done.71 = f32[7,1024]{1,0:T(8,128)S(1)} collective-permute-done((f32[7,1024]{1,0:T(8,128)S(1)}, f32[7,1024]{1,0:T(8,128)S(1)}, u32[]{:S(2)}, u32[]{:S(2)}) %collective-permute-start.71) | collective-permute-done | bytes 28704 | tf_op jit(solution)/shard_map/ppermute | solution.py:92
  716.1 7.3 collective-permute-start.40
  725.4 8.8 %collective-permute-done.30 = bf16[1024,256]{1,0:T(8,128)(2,1)S(1)} collective-permute-done((bf16[1024,256]{1,0:T(8,128)(2,1)S(1)}, bf16[1024,256]{1,0:T(8,128)(2,1)S(1)}, u32[]{:S(2)}, u32[]{:S(2)}) %collective-permute-start.30) | collective-permute-done | bytes 524320 | tf_op jit(solution)/shard_map/ppermute | solution.py:39
  734.4 10.5 %collective-permute-done.38 = bf16[1024,256]{1,0:T(8,128)(2,1)S(1)} collective-permute-done((bf16[1024,256]{1,0:T(8,128)(2,1)S(1)}, bf16[1024,256]{1,0:T(8,128)(2,1)S(1)}, u32[]{:S(2)}, u32[]{:S(2)}) %collective-permute-start.38) | collective-permute-done | bytes 524320 | tf_op jit(solution)/shard_map/ppermute | solution.py:39
  749.8 6.4 collective-permute-done.45
  756.3 4.0 collective-permute-done.41
  762.1 9.2 %collective-permute-done.46 = bf16[128,768]{0,1:T(8,128)(2,1)S(1)} collective-permute-done((bf16[128,768]{0,1:T(8,128)(2,1)S(1)}, bf16[128,768]{0,1:T(8,128)(2,1)S(1)}, u32[]{:S(2)}, u32[]{:S(2)}) %collective-permute-start.46) | collective-permute-done | bytes 196640 | tf_op jit(solution)/shard_map/ppermute | solution.py:39
  772.2 4.6 collective-permute-done.42
  (657 shorter events, 312.4 us)
Async XLA Ops:
  15.5 41.5 %collective-permute-start.5 = (bf16[3,1024]{0,1:T(8,128)(2,1)}, bf16[3,1024]{0,1:T(8,128)(2,1)S(1)}, u32[]{:S(2)}, u32[]{:S(2)}) collective-permute-start(bf16[3,1024]{0,1:T(8,128)(2,1)} %slice.225), channel_id=1, source_target_pairs={{0,4},{4,8},{8,12},{12,16},{16,20},{20,24},{24,28},{1,5},{5,9},{9,... | collective-permute-start | bytes 18440 | tf_op jit(solution)/shard_map/ppermute | solution.py:36
  22.1 76.1 %collective-permute-start.6 = (bf16[128,768]{0,1:T(8,128)(2,1)}, bf16[128,768]{0,1:T(8,128)(2,1)}, u32[]{:S(2)}, u32[]{:S(2)}) collective-permute-start(bf16[128,768]{0,1:T(8,128)(2,1)} %constant_dynamic-slice_fusion.24), channel_id=1, source_target_pairs={{0,2},{1,3},{2,0},{3,1},{4,6},{5,7},{6,4},{7,5},{8,10},{9,11},{10,... | collective-permute-start | bytes 589832 | tf_op jit(solution)/shard_map/ppermute | solution.py:39
  25.5 41.4 %collective-permute-start.10 = (f32[2,1024]{1,0:T(2,128)S(1)}, f32[2,1024]{1,0:T(2,128)S(1)}, u32[]{:S(2)}, u32[]{:S(2)}) collective-permute-start(f32[2,1024]{1,0:T(2,128)S(1)} %get-tuple-element.134), channel_id=1, source_target_pairs={{0,2},{1,3},{2,0},{3,1},{4,6},{5,7},{6,4},{7,5},{8,10},{9,11},{10,... | collective-permute-start | bytes 24584 | tf_op jit(solution)/shard_map/ppermute | solution.py:39
  29.8 68.9 %collective-permute-start = (bf16[128,1024]{1,0:T(8,128)(2,1)}, bf16[128,1024]{1,0:T(8,128)(2,1)}, u32[]{:S(2)}, u32[]{:S(2)}) collective-permute-start(bf16[128,1024]{1,0:T(8,128)(2,1)} %constant_dynamic-slice_fusion.25), channel_id=1, source_target_pairs={{0,2},{1,3},{2,0},{3,1},{4,6},{5,7},{6,4},{7,5},{8,10},{9,11},{10,... | collective-permute-start | bytes 786440 | tf_op jit(solution)/shard_map/ppermute | solution.py:39
  32.6 45.7 %collective-permute-start.4 = (bf16[32,256]{1,0:T(8,128)(2,1)S(1)}, bf16[32,256]{1,0:T(8,128)(2,1)}, u32[]{:S(2)}, u32[]{:S(2)}) collective-permute-start(bf16[32,256]{1,0:T(8,128)(2,1)S(1)} %copy-done.125), channel_id=1, source_target_pairs={{0,2},{1,3},{2,0},{3,1},{4,6},{5,7},{6,4},{7,5},{8,10},{9,11},{10,... | collective-permute-start | bytes 49160 | tf_op jit(solution)/shard_map/ppermute | solution.py:39
  57.0 39.6 %collective-permute-start.25 = (bf16[88,1024]{1,0:T(8,128)(2,1)}, bf16[88,1024]{1,0:T(8,128)(2,1)}, u32[]{:S(2)}, u32[]{:S(2)}) collective-permute-start(bf16[88,1024]{1,0:T(8,128)(2,1)} %constant_dynamic-slice_fusion.18), channel_id=1, source_target_pairs={{0,2},{1,3},{2,0},{3,1},{4,6},{5,7},{6,4},{7,5},{8,10},{9,11},{10,... | collective-permute-start | bytes 540680 | tf_op jit(solution)/shard_map/ppermute | solution.py:39
  77.5 13.2 %collective-permute-start.16 = (bf16[32,1024]{1,0:T(8,128)(2,1)S(1)}, bf16[32,1024]{1,0:T(8,128)(2,1)S(1)}, u32[]{:S(2)}, u32[]{:S(2)}) collective-permute-start(bf16[32,1024]{1,0:T(8,128)(2,1)S(1)} %copy-done.107), channel_id=1, source_target_pairs={{0,2},{1,3},{2,0},{3,1},{4,6},{5,7},{6,4},{7,5},{8,10},{9,11},{10,... | collective-permute-start | bytes 196616 | tf_op jit(solution)/shard_map/ppermute | solution.py:39
  78.4 25.6 %collective-permute-start.21 = (bf16[128,1408]{0,1:T(8,128)(2,1)S(1)}, bf16[128,1408]{0,1:T(8,128)(2,1)S(1)}, u32[]{:S(2)}, u32[]{:S(2)}) collective-permute-start(bf16[128,1408]{0,1:T(8,128)(2,1)S(1)} %copy-done.93), channel_id=1, source_target_pairs={{0,2},{1,3},{2,0},{3,1},{4,6},{5,7},{6,4},{7,5},{8,10},{9,11},{10,... | collective-permute-start | bytes 1081352 | tf_op jit(solution)/shard_map/ppermute | solution.py:39
  95.0 5.0 collective-permute-start.18
  96.6 5.8 collective-permute-start.26
  98.1 7.3 collective-permute-start.7
  98.7 8.4 %collective-permute-start.1 = (bf16[1,128,1024]{2,1,0:T(8,128)(2,1)}, bf16[1,128,1024]{2,1,0:T(8,128)(2,1)S(1)}, u32[]{:S(2)}, u32[]{:S(2)}) collective-permute-start(bf16[1,128,1024]{2,1,0:T(8,128)(2,1)} %bitcast.6), channel_id=1, source_target_pairs={{0,16},{4,20},{8,24},{12,28},{16,0},{20,4},{24,8},{28,12},{1,17},{... | collective-permute-start | bytes 786440 | tf_op jit(solution)/shard_map/ppermute | solution.py:32
  100.1 10.4 %collective-permute-start.19 = (bf16[4,32,1024]{2,1,0:T(8,128)(2,1)S(1)}, bf16[4,32,1024]{2,1,0:T(8,128)(2,1)S(1)}, u32[]{:S(2)}, u32[]{:S(2)}) collective-permute-start(bf16[4,32,1024]{2,1,0:T(8,128)(2,1)S(1)} %bitcast.629), channel_id=1, source_target_pairs={{0,4},{4,0},{8,12},{12,8},{16,20},{20,16},{24,28},{28,24},{1,5},{5... | collective-permute-start | bytes 786440 | tf_op jit(solution)/shard_map/ppermute | solution.py:32
  103.4 11.4 %collective-permute-start.27 = (bf16[2,88,1024]{2,1,0:T(8,128)(2,1)S(1)}, bf16[2,88,1024]{2,1,0:T(8,128)(2,1)S(1)}, u32[]{:S(2)}, u32[]{:S(2)}) collective-permute-start(bf16[2,88,1024]{2,1,0:T(8,128)(2,1)S(1)} %pad_maximum_fusion.28), channel_id=1, source_target_pairs={{0,16},{4,20},{8,24},{12,28},{16,0},{20,4},{24,8},{28,12},{1,17},{... | collective-permute-start | bytes 1081352 | tf_op jit(solution)/shard_map/ppermute | solution.py:32
  103.9 18.6 %collective-permute-start.22 = (bf16[1,128,1408]{1,2,0:T(8,128)(2,1)S(1)}, bf16[1,128,1408]{1,2,0:T(8,128)(2,1)S(1)}, u32[]{:S(2)}, u32[]{:S(2)}) collective-permute-start(bf16[1,128,1408]{1,2,0:T(8,128)(2,1)S(1)} %bitcast.639), channel_id=1, source_target_pairs={{0,16},{4,20},{8,24},{12,28},{16,0},{20,4},{24,8},{28,12},{1,17},{... | collective-permute-start | bytes 1081352 | tf_op jit(solution)/shard_map/ppermute | solution.py:32
  106.5 22.7 %collective-permute-start.8 = (bf16[2,128,768]{1,2,0:T(8,128)(2,1)S(1)}, bf16[2,128,768]{1,2,0:T(8,128)(2,1)S(1)}, u32[]{:S(2)}, u32[]{:S(2)}) collective-permute-start(bf16[2,128,768]{1,2,0:T(8,128)(2,1)S(1)} %pad_maximum_fusion.27), channel_id=1, source_target_pairs={{0,16},{4,20},{8,24},{12,28},{16,0},{20,4},{24,8},{28,12},{1,17},{... | collective-permute-start | bytes 1179656 | tf_op jit(solution)/shard_map/ppermute | solution.py:32
  108.9 21.5 %collective-permute-start.2 = (bf16[2,128,1024]{2,1,0:T(8,128)(2,1)}, bf16[2,128,1024]{2,1,0:T(8,128)(2,1)}, u32[]{:S(2)}, u32[]{:S(2)}) collective-permute-start(bf16[2,128,1024]{2,1,0:T(8,128)(2,1)} %pad_maximum_fusion.25), channel_id=1, source_target_pairs={{0,8},{4,12},{8,0},{12,4},{16,24},{20,28},{24,16},{28,20},{1,9},{5... | collective-permute-start | bytes 1572872 | tf_op jit(solution)/shard_map/ppermute | solution.py:32
  115.8 151.8 %collective-permute-start.28 = (bf16[4,88,1024]{2,1,0:T(8,128)(2,1)}, bf16[4,88,1024]{2,1,0:T(8,128)(2,1)}, u32[]{:S(2)}, u32[]{:S(2)}) collective-permute-start(bf16[4,88,1024]{2,1,0:T(8,128)(2,1)} %bitcast.79), channel_id=1, source_target_pairs={{0,4},{4,0},{8,12},{12,8},{16,20},{20,16},{24,28},{28,24},{1,5},{5... | collective-permute-start | bytes 2162696 | tf_op jit(solution)/shard_map/ppermute | solution.py:32
  123.5 15.0 %collective-permute-start.23 = (bf16[2,128,1408]{1,2,0:T(8,128)(2,1)}, bf16[2,128,1408]{1,2,0:T(8,128)(2,1)}, u32[]{:S(2)}, u32[]{:S(2)}) collective-permute-start(bf16[2,128,1408]{1,2,0:T(8,128)(2,1)} %pad_maximum_fusion.20), channel_id=1, source_target_pairs={{0,8},{4,12},{8,0},{12,4},{16,24},{20,28},{24,16},{28,20},{1,9},{5... | collective-permute-start | bytes 2162696 | tf_op jit(solution)/shard_map/ppermute | solution.py:32
  130.5 11.0 %collective-permute-start.9 = (bf16[4,128,768]{2,1,0:T(8,128)(2,1)}, bf16[4,128,768]{2,1,0:T(8,128)(2,1)}, u32[]{:S(2)}, u32[]{:S(2)}) collective-permute-start(bf16[4,128,768]{2,1,0:T(8,128)(2,1)} %copy.246), channel_id=1, source_target_pairs={{0,4},{4,0},{8,12},{12,8},{16,20},{20,16},{24,28},{28,24},{1,5},{5... | collective-permute-start | bytes 2359304 | tf_op jit(solution)/shard_map/ppermute | solution.py:32
  132.6 71.4 %collective-permute-start.3 = (bf16[4,128,1024]{2,1,0:T(8,128)(2,1)}, bf16[4,128,1024]{2,1,0:T(8,128)(2,1)}, u32[]{:S(2)}, u32[]{:S(2)}) collective-permute-start(bf16[4,128,1024]{2,1,0:T(8,128)(2,1)} %bitcast.10), channel_id=1, source_target_pairs={{0,4},{4,0},{8,12},{12,8},{16,20},{20,16},{24,28},{28,24},{1,5},{5... | collective-permute-start | bytes 3145736 | tf_op jit(solution)/shard_map/ppermute | solution.py:32
  141.4 134.9 %collective-permute-start.24 = (bf16[4,128,1408]{2,1,0:T(8,128)(2,1)}, bf16[4,128,1408]{2,1,0:T(8,128)(2,1)}, u32[]{:S(2)}, u32[]{:S(2)}) collective-permute-start(bf16[4,128,1408]{2,1,0:T(8,128)(2,1)} %bitcast.586), channel_id=1, source_target_pairs={{0,4},{4,0},{8,12},{12,8},{16,20},{20,16},{24,28},{28,24},{1,5},{5... | collective-permute-start | bytes 4325384 | tf_op jit(solution)/shard_map/ppermute | solution.py:32
  190.6 11.7 %collective-permute-start.13 = (f32[4,128,128]{2,1,0:T(8,128)S(1)}, f32[4,128,128]{2,1,0:T(8,128)S(1)}, u32[]{:S(2)}, u32[]{:S(2)}) collective-permute-start(f32[4,128,128]{2,1,0:T(8,128)S(1)} %fusion.59), channel_id=1, source_target_pairs={{0,4},{4,0},{8,12},{12,8},{16,20},{20,16},{24,28},{28,24},{1,5},{5... | collective-permute-start | bytes 786440 | tf_op jit(solution)/shard_map/ppermute | solution.py:32
  202.5 26.1 %collective-permute-start.14 = (f32[4,128,128]{2,1,0:T(8,128)S(1)}, f32[4,128,128]{2,1,0:T(8,128)S(1)}, u32[]{:S(2)}, u32[]{:S(2)}) collective-permute-start(f32[4,128,128]{2,1,0:T(8,128)S(1)} %select_add_fusion.3), channel_id=1, source_target_pairs={{0,8},{4,12},{8,0},{12,4},{16,24},{20,28},{24,16},{28,20},{1,9},{5... | collective-permute-start | bytes 786440 | tf_op jit(solution)/shard_map/ppermute | solution.py:32
  229.4 31.5 %collective-permute-start.15 = (f32[4,128,128]{2,1,0:T(8,128)}, f32[4,128,128]{2,1,0:T(8,128)}, u32[]{:S(2)}, u32[]{:S(2)}) collective-permute-start(f32[4,128,128]{2,1,0:T(8,128)} %select_add_fusion.2), channel_id=1, source_target_pairs={{0,16},{4,20},{8,24},{12,28},{16,0},{20,4},{24,8},{28,12},{1,17},{... | collective-permute-start | bytes 786440 | tf_op jit(solution)/shard_map/ppermute | solution.py:32
  267.5 47.4 %collective-permute-start.20 = (bf16[1024,1024]{0,1:T(8,128)(2,1)}, bf16[1024,1024]{0,1:T(8,128)(2,1)}, u32[]{:S(2)}, u32[]{:S(2)}) collective-permute-start(bf16[1024,1024]{0,1:T(8,128)(2,1)} %convolution_convert_fusion.6), channel_id=1, source_target_pairs={{0,1},{1,0},{2,3},{3,2},{4,5},{5,4},{6,7},{7,6},{8,9},{9,8},{10,11... | collective-permute-start | bytes 6291464 | tf_op jit(solution)/shard_map/ppermute | solution.py:43
  353.6 56.9 %collective-permute-start.31 = (bf16[1024,1024]{0,1:T(8,128)(2,1)}, bf16[1024,1024]{0,1:T(8,128)(2,1)}, u32[]{:S(2)}, u32[]{:S(2)}) collective-permute-start(bf16[1024,1024]{0,1:T(8,128)(2,1)} %add_convert_fusion), channel_id=1, source_target_pairs={{0,1},{1,0},{2,3},{3,2},{4,5},{5,4},{6,7},{7,6},{8,9},{9,8},{10,11... | collective-permute-start | bytes 6291464 | tf_op jit(solution)/shard_map/ppermute | solution.py:43
  370.0 28.4 %collective-permute-start.55 = (bf16[2,2,128,1408]{2,3,0,1:T(8,128)(2,1)}, bf16[2,2,128,1408]{2,3,0,1:T(8,128)(2,1)}, u32[]{:S(2)}, u32[]{:S(2)}) collective-permute-start(bf16[2,2,128,1408]{2,3,0,1:T(8,128)(2,1)} %bitcast.625), channel_id=1, source_target_pairs={{0,4},{4,0},{8,12},{12,8},{16,20},{20,16},{24,28},{28,24},{1,5},{5... | collective-permute-start | bytes 4325384 | tf_op jit(solution)/shard_map/ppermute | solution.py:32
  382.9 19.0 %collective-permute-start.51 = (bf16[2,2,128,1408]{2,3,1,0:T(8,128)(2,1)}, bf16[2,2,128,1408]{2,3,1,0:T(8,128)(2,1)}, u32[]{:S(2)}, u32[]{:S(2)}) collective-permute-start(bf16[2,2,128,1408]{2,3,1,0:T(8,128)(2,1)} %bitcast.627), channel_id=1, source_target_pairs={{0,4},{4,0},{8,12},{12,8},{16,20},{20,16},{24,28},{28,24},{1,5},{5... | collective-permute-start | bytes 4325384 | tf_op jit(solution)/shard_map/ppermute | solution.py:32
  388.4 17.5 %collective-permute-start.59 = (bf16[2,2,128,1408]{2,3,1,0:T(8,128)(2,1)}, bf16[2,2,128,1408]{2,3,1,0:T(8,128)(2,1)}, u32[]{:S(2)}, u32[]{:S(2)}) collective-permute-start(bf16[2,2,128,1408]{2,3,1,0:T(8,128)(2,1)} %bitcast.626), channel_id=1, source_target_pairs={{0,4},{4,0},{8,12},{12,8},{16,20},{20,16},{24,28},{28,24},{1,5},{5... | collective-permute-start | bytes 4325384 | tf_op jit(solution)/shard_map/ppermute | solution.py:32
  401.3 112.6 %collective-permute-start.56 = (bf16[2,128,1408]{1,2,0:T(8,128)(2,1)}, bf16[2,128,1408]{1,2,0:T(8,128)(2,1)}, u32[]{:S(2)}, u32[]{:S(2)}) collective-permute-start(bf16[2,128,1408]{1,2,0:T(8,128)(2,1)} %fusion.62), channel_id=1, source_target_pairs={{0,8},{4,12},{8,0},{12,4},{16,24},{20,28},{24,16},{28,20},{1,9},{5... | collective-permute-start | bytes 2162696 | tf_op jit(solution)/shard_map/ppermute | solution.py:32
  404.6 111.8 %collective-permute-start.52 = (bf16[2,128,1408]{1,2,0:T(8,128)(2,1)}, bf16[2,128,1408]{1,2,0:T(8,128)(2,1)}, u32[]{:S(2)}, u32[]{:S(2)}) collective-permute-start(bf16[2,128,1408]{1,2,0:T(8,128)(2,1)} %fusion.61), channel_id=1, source_target_pairs={{0,16},{4,20},{8,24},{12,28},{16,0},{20,4},{24,8},{28,12},{1,17},{... | collective-permute-start | bytes 2162696 | tf_op jit(solution)/shard_map/ppermute | solution.py:32
  409.4 109.4 %collective-permute-start.60 = (bf16[2,128,1408]{1,2,0:T(8,128)(2,1)}, bf16[2,128,1408]{1,2,0:T(8,128)(2,1)}, u32[]{:S(2)}, u32[]{:S(2)}) collective-permute-start(bf16[2,128,1408]{1,2,0:T(8,128)(2,1)} %fusion.63), channel_id=1, source_target_pairs={{0,16},{4,20},{8,24},{12,28},{16,0},{20,4},{24,8},{28,12},{1,17},{... | collective-permute-start | bytes 2162696 | tf_op jit(solution)/shard_map/ppermute | solution.py:32
  458.2 76.7 %collective-permute-start.33 = (f32[4,128,128]{2,1,0:T(8,128)}, f32[4,128,128]{2,1,0:T(8,128)}, u32[]{:S(2)}, u32[]{:S(2)}) collective-permute-start(f32[4,128,128]{2,1,0:T(8,128)} %fusion.58), channel_id=1, source_target_pairs={{0,4},{4,0},{8,12},{12,8},{16,20},{20,16},{24,28},{28,24},{1,5},{5... | collective-permute-start | bytes 786440 | tf_op jit(solution)/shard_map/ppermute | solution.py:32
  499.2 14.6 %collective-permute-start.63 = (f32[32,512]{1,0:T(8,128)S(1)}, f32[32,512]{1,0:T(8,128)S(1)}, u32[]{:S(2)}, u32[]{:S(2)}) collective-permute-start(f32[32,512]{1,0:T(8,128)S(1)} %bitcast_dynamic-update-slice_fusion), channel_id=1, source_target_pairs={{0,4},{4,0},{8,12},{12,8},{16,20},{20,16},{24,28},{28,24},{1,5},{5... | collective-permute-start | bytes 196616 | tf_op jit(solution)/shard_map/ppermute | solution.py:32
  513.8 199.8 %collective-permute-start.39 = (bf16[2,2,128,2048]{3,2,1,0:T(8,128)(2,1)}, bf16[2,2,128,2048]{3,2,1,0:T(8,128)(2,1)}, u32[]{:S(2)}, u32[]{:S(2)}) collective-permute-start(bf16[2,2,128,2048]{3,2,1,0:T(8,128)(2,1)} %dynamic-slice_bitcast_fusion), channel_id=1, source_target_pairs={{0,4},{4,0},{8,12},{12,8},{16,20},{20,16},{24,28},{28,24},{1,5},{5... | collective-permute-start | bytes 6291464 | tf_op jit(solution)/shard_map/ppermute | solution.py:32
  513.9 43.3 %collective-permute-start.47 = (bf16[2,2,128,512]{2,3,0,1:T(8,128)(2,1)}, bf16[2,2,128,512]{2,3,0,1:T(8,128)(2,1)S(1)}, u32[]{:S(2)}, u32[]{:S(2)}) collective-permute-start(bf16[2,2,128,512]{2,3,0,1:T(8,128)(2,1)} %bitcast.638), channel_id=1, source_target_pairs={{0,4},{4,0},{8,12},{12,8},{16,20},{20,16},{24,28},{28,24},{1,5},{5... | collective-permute-start | bytes 1572872 | tf_op jit(solution)/shard_map/ppermute | solution.py:32
  516.4 20.2 %collective-permute-start.57 = (bf16[128,1408]{0,1:T(8,128)(2,1)S(1)}, bf16[128,1408]{0,1:T(8,128)(2,1)S(1)}, u32[]{:S(2)}, u32[]{:S(2)}) collective-permute-start(bf16[128,1408]{0,1:T(8,128)(2,1)S(1)} %fusion.69), channel_id=1, source_target_pairs={{0,16},{4,20},{8,24},{12,28},{16,0},{20,4},{24,8},{28,12},{1,17},{... | collective-permute-start | bytes 1081352 | tf_op jit(solution)/shard_map/ppermute | solution.py:32
  523.2 5.0 collective-permute-start.65
  532.8 11.4 %collective-permute-start.53 = (bf16[128,1408]{0,1:T(8,128)(2,1)S(1)}, bf16[128,1408]{0,1:T(8,128)(2,1)S(1)}, u32[]{:S(2)}, u32[]{:S(2)}) collective-permute-start(bf16[128,1408]{0,1:T(8,128)(2,1)S(1)} %fusion.68), channel_id=1, source_target_pairs={{0,8},{4,12},{8,0},{12,4},{16,24},{20,28},{24,16},{28,20},{1,9},{5... | collective-permute-start | bytes 1081352 | tf_op jit(solution)/shard_map/ppermute | solution.py:32
  534.9 16.8 %collective-permute-start.61 = (bf16[128,1408]{0,1:T(8,128)(2,1)S(1)}, bf16[128,1408]{0,1:T(8,128)(2,1)S(1)}, u32[]{:S(2)}, u32[]{:S(2)}) collective-permute-start(bf16[128,1408]{0,1:T(8,128)(2,1)S(1)} %fusion.70), channel_id=1, source_target_pairs={{0,8},{4,12},{8,0},{12,4},{16,24},{20,28},{24,16},{28,20},{1,9},{5... | collective-permute-start | bytes 1081352 | tf_op jit(solution)/shard_map/ppermute | solution.py:32
  536.6 17.9 %collective-permute-start.34 = (f32[4,128,128]{2,1,0:T(8,128)S(1)}, f32[4,128,128]{2,1,0:T(8,128)S(1)}, u32[]{:S(2)}, u32[]{:S(2)}) collective-permute-start(f32[4,128,128]{2,1,0:T(8,128)S(1)} %select_add_fusion.1), channel_id=1, source_target_pairs={{0,8},{4,12},{8,0},{12,4},{16,24},{20,28},{24,16},{28,20},{1,9},{5... | collective-permute-start | bytes 786440 | tf_op jit(solution)/shard_map/ppermute | solution.py:32
  544.2 15.1 %collective-permute-start.58 = (bf16[128,704]{0,1:T(8,128)(2,1)S(1)}, bf16[128,704]{0,1:T(8,128)(2,1)S(1)}, u32[]{:S(2)}, u32[]{:S(2)}) collective-permute-start(bf16[128,704]{0,1:T(8,128)(2,1)S(1)} %slice.336), channel_id=1, source_target_pairs={{0,2},{1,3},{2,0},{3,1},{4,6},{5,7},{6,4},{7,5},{8,10},{9,11},{10,... | collective-permute-start | bytes 540680 | tf_op jit(solution)/shard_map/ppermute | solution.py:39
  551.7 14.2 %collective-permute-start.54 = (bf16[128,704]{0,1:T(8,128)(2,1)S(1)}, bf16[128,704]{0,1:T(8,128)(2,1)S(1)}, u32[]{:S(2)}, u32[]{:S(2)}) collective-permute-start(bf16[128,704]{0,1:T(8,128)(2,1)S(1)} %slice.337), channel_id=1, source_target_pairs={{0,2},{1,3},{2,0},{3,1},{4,6},{5,7},{6,4},{7,5},{8,10},{9,11},{10,... | collective-permute-start | bytes 540680 | tf_op jit(solution)/shard_map/ppermute | solution.py:39
  554.5 13.4 %collective-permute-start.62 = (bf16[128,704]{0,1:T(8,128)(2,1)S(1)}, bf16[128,704]{0,1:T(8,128)(2,1)S(1)}, u32[]{:S(2)}, u32[]{:S(2)}) collective-permute-start(bf16[128,704]{0,1:T(8,128)(2,1)S(1)} %slice.335), channel_id=1, source_target_pairs={{0,2},{1,3},{2,0},{3,1},{4,6},{5,7},{6,4},{7,5},{8,10},{9,11},{10,... | collective-permute-start | bytes 540680 | tf_op jit(solution)/shard_map/ppermute | solution.py:39
  557.2 11.5 %collective-permute-start.35 = (f32[4,128,128]{2,1,0:T(8,128)S(1)}, f32[4,128,128]{2,1,0:T(8,128)S(1)}, u32[]{:S(2)}, u32[]{:S(2)}) collective-permute-start(f32[4,128,128]{2,1,0:T(8,128)S(1)} %select_add_fusion), channel_id=1, source_target_pairs={{0,16},{4,20},{8,24},{12,28},{16,0},{20,4},{24,8},{28,12},{1,17},{... | collective-permute-start | bytes 786440 | tf_op jit(solution)/shard_map/ppermute | solution.py:32
  559.3 52.0 %collective-permute-start.48 = (bf16[2,128,512]{1,2,0:T(8,128)(2,1)}, bf16[2,128,512]{1,2,0:T(8,128)(2,1)S(1)}, u32[]{:S(2)}, u32[]{:S(2)}) collective-permute-start(bf16[2,128,512]{1,2,0:T(8,128)(2,1)} %fusion.76), channel_id=1, source_target_pairs={{0,8},{4,12},{8,0},{12,4},{16,24},{20,28},{24,16},{28,20},{1,9},{5... | collective-permute-start | bytes 786440 | tf_op jit(solution)/shard_map/ppermute | solution.py:32
  598.8 14.3 %collective-permute-start.36 = (f32[3,1024]{0,1:T(8,128)}, f32[3,1024]{0,1:T(8,128)}, u32[]{:S(2)}, u32[]{:S(2)}) collective-permute-start(f32[3,1024]{0,1:T(8,128)} %pad_add_fusion.1), channel_id=1, source_target_pairs={{4,0},{8,4},{12,8},{16,12},{20,16},{24,20},{28,24},{5,1},{9,5},{13... | collective-permute-start | bytes 36872 | tf_op jit(solution)/shard_map/ppermute | solution.py:36
  611.3 27.6 %collective-permute-start.49 = (bf16[128,512]{0,1:T(8,128)(2,1)S(1)}, bf16[128,512]{0,1:T(8,128)(2,1)S(1)}, u32[]{:S(2)}, u32[]{:S(2)}) collective-permute-start(bf16[128,512]{0,1:T(8,128)(2,1)S(1)} %fusion.80), channel_id=1, source_target_pairs={{0,16},{4,20},{8,24},{12,28},{16,0},{20,4},{24,8},{28,12},{1,17},{... | collective-permute-start | bytes 393224 | tf_op jit(solution)/shard_map/ppermute | solution.py:32
  627.9 47.9 %collective-permute-start.29 = (bf16[1024,2,256]{2,0,1:T(8,128)(2,1)}, bf16[1024,2,256]{2,0,1:T(8,128)(2,1)}, u32[]{:S(2)}, u32[]{:S(2)}) collective-permute-start(bf16[1024,2,256]{2,0,1:T(8,128)(2,1)} %bitcast.85), channel_id=1, source_target_pairs={{0,1},{1,0},{2,3},{3,2},{4,5},{5,4},{6,7},{7,6},{8,9},{9,8},{10,11... | collective-permute-start | bytes 3145736 | tf_op jit(solution)/shard_map/ppermute | solution.py:43
  636.9 45.2 %collective-permute-start.37 = (bf16[1024,2,256]{2,0,1:T(8,128)(2,1)}, bf16[1024,2,256]{2,0,1:T(8,128)(2,1)}, u32[]{:S(2)}, u32[]{:S(2)}) collective-permute-start(bf16[1024,2,256]{2,0,1:T(8,128)(2,1)} %bitcast.134), channel_id=1, source_target_pairs={{0,1},{1,0},{2,3},{3,2},{4,5},{5,4},{6,7},{7,6},{8,9},{9,8},{10,11... | collective-permute-start | bytes 3145736 | tf_op jit(solution)/shard_map/ppermute | solution.py:43
  639.0 36.1 %collective-permute-start.50 = (bf16[128,256]{0,1:T(8,128)(2,1)S(1)}, bf16[128,256]{0,1:T(8,128)(2,1)S(1)}, u32[]{:S(2)}, u32[]{:S(2)}) collective-permute-start(bf16[128,256]{0,1:T(8,128)(2,1)S(1)} %slice.338), channel_id=1, source_target_pairs={{0,2},{1,3},{2,0},{3,1},{4,6},{5,7},{6,4},{7,5},{8,10},{9,11},{10,... | collective-permute-start | bytes 196616 | tf_op jit(solution)/shard_map/ppermute | solution.py:39
  643.6 79.8 %collective-permute-start.43 = (bf16[2,2,128,1536]{2,3,1,0:T(8,128)(2,1)}, bf16[2,2,128,1536]{2,3,1,0:T(8,128)(2,1)}, u32[]{:S(2)}, u32[]{:S(2)}) collective-permute-start(bf16[2,2,128,1536]{2,3,1,0:T(8,128)(2,1)} %bitcast.621), channel_id=1, source_target_pairs={{0,4},{4,0},{8,12},{12,8},{16,20},{20,16},{24,28},{28,24},{1,5},{5... | collective-permute-start | bytes 4718600 | tf_op jit(solution)/shard_map/ppermute | solution.py:32
  691.9 5.7 collective-permute-start.72
  694.2 17.6 %collective-permute-start.71 = (f32[7,1024]{1,0:T(8,128)S(1)}, f32[7,1024]{1,0:T(8,128)S(1)}, u32[]{:S(2)}, u32[]{:S(2)}) collective-permute-start(f32[7,1024]{1,0:T(8,128)S(1)} %add.608), channel_id=1, source_target_pairs={{0,2},{1,3},{2,0},{3,1},{4,6},{5,7},{6,4},{7,5},{8,10},{9,11},{10,... | collective-permute-start | bytes 86024 | tf_op jit(solution)/shard_map/ppermute | solution.py:92
  696.7 15.1 %collective-permute-start.70 = (f32[7,1024]{1,0:T(8,128)S(1)}, f32[7,1024]{1,0:T(8,128)S(1)}, u32[]{:S(2)}, u32[]{:S(2)}) collective-permute-start(f32[7,1024]{1,0:T(8,128)S(1)} %add.608), channel_id=1, source_target_pairs={{0,1},{1,2},{2,3},{3,0},{4,5},{5,6},{6,7},{7,4},{8,9},{9,10},{10,1... | collective-permute-start | bytes 86024 | tf_op jit(solution)/shard_map/ppermute | solution.py:92
  697.6 36.6 %collective-permute-start.30 = (bf16[1024,256]{1,0:T(8,128)(2,1)S(1)}, bf16[1024,256]{1,0:T(8,128)(2,1)S(1)}, u32[]{:S(2)}, u32[]{:S(2)}) collective-permute-start(bf16[1024,256]{1,0:T(8,128)(2,1)S(1)} %fusion.64), channel_id=1, source_target_pairs={{0,2},{1,3},{2,0},{3,1},{4,6},{5,7},{6,4},{7,5},{8,10},{9,11},{10,... | collective-permute-start | bytes 1572872 | tf_op jit(solution)/shard_map/ppermute | solution.py:39
  711.8 33.1 %collective-permute-start.38 = (bf16[1024,256]{1,0:T(8,128)(2,1)S(1)}, bf16[1024,256]{1,0:T(8,128)(2,1)S(1)}, u32[]{:S(2)}, u32[]{:S(2)}) collective-permute-start(bf16[1024,256]{1,0:T(8,128)(2,1)S(1)} %fusion.65), channel_id=1, source_target_pairs={{0,2},{1,3},{2,0},{3,1},{4,6},{5,7},{6,4},{7,5},{8,10},{9,11},{10,... | collective-permute-start | bytes 1572872 | tf_op jit(solution)/shard_map/ppermute | solution.py:39
  716.1 28.9 %collective-permute-start.40 = (bf16[2,128,2048]{2,1,0:T(8,128)(2,1)S(1)}, bf16[2,128,2048]{2,1,0:T(8,128)(2,1)S(1)}, u32[]{:S(2)}, u32[]{:S(2)}) collective-permute-start(bf16[2,128,2048]{2,1,0:T(8,128)(2,1)S(1)} %fusion.51), channel_id=1, source_target_pairs={{0,8},{4,12},{8,0},{12,4},{16,24},{20,28},{24,16},{28,20},{1,9},{5... | collective-permute-start | bytes 3145736 | tf_op jit(solution)/shard_map/ppermute | solution.py:32
  725.3 20.1 %collective-permute-start.44 = (bf16[2,128,1536]{1,2,0:T(8,128)(2,1)S(1)}, bf16[2,128,1536]{1,2,0:T(8,128)(2,1)S(1)}, u32[]{:S(2)}, u32[]{:S(2)}) collective-permute-start(bf16[2,128,1536]{1,2,0:T(8,128)(2,1)S(1)} %fusion.60), channel_id=1, source_target_pairs={{0,16},{4,20},{8,24},{12,28},{16,0},{20,4},{24,8},{28,12},{1,17},{... | collective-permute-start | bytes 2359304 | tf_op jit(solution)/shard_map/ppermute | solution.py:32
  745.6 10.6 %collective-permute-start.45 = (bf16[128,1536]{0,1:T(8,128)(2,1)S(1)}, bf16[128,1536]{0,1:T(8,128)(2,1)S(1)}, u32[]{:S(2)}, u32[]{:S(2)}) collective-permute-start(bf16[128,1536]{0,1:T(8,128)(2,1)S(1)} %fusion.67), channel_id=1, source_target_pairs={{0,8},{4,12},{8,0},{12,4},{16,24},{20,28},{24,16},{28,20},{1,9},{5... | collective-permute-start | bytes 1179656 | tf_op jit(solution)/shard_map/ppermute | solution.py:32
  747.3 13.1 %collective-permute-start.41 = (bf16[128,2048]{1,0:T(8,128)(2,1)S(1)}, bf16[128,2048]{1,0:T(8,128)(2,1)S(1)}, u32[]{:S(2)}, u32[]{:S(2)}) collective-permute-start(bf16[128,2048]{1,0:T(8,128)(2,1)S(1)} %fusion.66), channel_id=1, source_target_pairs={{0,16},{4,20},{8,24},{12,28},{16,0},{20,4},{24,8},{28,12},{1,17},{... | collective-permute-start | bytes 1572872 | tf_op jit(solution)/shard_map/ppermute | solution.py:32
  756.2 15.0 %collective-permute-start.46 = (bf16[128,768]{0,1:T(8,128)(2,1)S(1)}, bf16[128,768]{0,1:T(8,128)(2,1)S(1)}, u32[]{:S(2)}, u32[]{:S(2)}) collective-permute-start(bf16[128,768]{0,1:T(8,128)(2,1)S(1)} %slice.334), channel_id=1, source_target_pairs={{0,2},{1,3},{2,0},{3,1},{4,6},{5,7},{6,4},{7,5},{8,10},{9,11},{10,... | collective-permute-start | bytes 589832 | tf_op jit(solution)/shard_map/ppermute | solution.py:39
  760.5 16.2 %collective-permute-start.42 = (bf16[128,1024]{1,0:T(8,128)(2,1)S(1)}, bf16[128,1024]{1,0:T(8,128)(2,1)S(1)}, u32[]{:S(2)}, u32[]{:S(2)}) collective-permute-start(bf16[128,1024]{1,0:T(8,128)(2,1)S(1)} %slice.333), channel_id=1, source_target_pairs={{0,2},{1,3},{2,0},{3,1},{4,6},{5,7},{6,4},{7,5},{8,10},{9,11},{10,... | collective-permute-start | bytes 786440 | tf_op jit(solution)/shard_map/ppermute | solution.py:39
  (160 other events, 2534.3 us)
